TPU v7x, 256 devices: a whole 4x4x8 slice. The times are simulated.
256 devices in a mesh: env: 2 (over x_lo), row: 8 (over y, core), col: 16 (over z, x_hi).
Axes of the slice: x: 4 (x_hi: 2, x_lo: 2; x = x_hi * 2 + x_lo), y: 4, z: 8, core: 2. Of those that a mesh axis runs over, the one named last changes fastest.
Arguments:
- adjoint_hat: float32 [2, 3, 2, 256, 256, 256], P('env', None, None, 'row', 'col'), may hold values from -6 to 6
- velocity: float32 [2, 3, 256, 256, 256], P('env', None, 'row', 'col'), may hold values from -6 to 6
- vorticity: float32 [2, 3, 256, 256, 256], P('env', None, 'row', 'col'), may hold values from -6 to 6
Outputs:
- adjoint_out: float32 [2, 3, 2, 256, 256, 256], P('env', None, None, 'row', 'col')
- controller_grad: float32 [3, 6], replicated
All inputs are finite; a program needn't handle non-finite values.
Results may differ from a plain program's by a relative error of at most 0.00027.
Values sent between devices are 32-bit elements; how exact they have to be, the bound alone decides.
A program may use at most 128 MiB of HBM per device.

v0:
```python
import math

import jax
import jax.numpy as jnp
from jax import lax
from jax.sharding import PartitionSpec as P

HIGHEST_PRECISION = lax.Precision.HIGHEST


def tables(length):
    indices = lax.iota(jnp.int32, length)
    product = indices[:, None] * indices[None, :] % length
    angles = product.astype(jnp.float32) * (2.0 * math.pi / length)
    norm_factor = 1.0 / math.sqrt(length)
    cosines = jnp.cos(angles) * norm_factor
    sines = jnp.sin(angles) * norm_factor
    backward = jnp.stack((jnp.stack((cosines, -sines)), jnp.stack((sines, cosines))))
    forward = jnp.stack((jnp.stack((cosines, sines)), jnp.stack((-sines, cosines))))
    real_back = jnp.stack((cosines, -sines))
    real_fwd = jnp.stack((cosines, -sines))
    return (backward, forward, real_back, real_fwd)


def contract(pattern, values, table):
    return jnp.einsum(pattern, values, table, precision=HIGHEST_PRECISION)


def inverse_pencil(spectra, backward, real_back, along_rows, along_cols):
    section = contract("fsabk,tsxk->ftabx", spectra, backward)
    arrived = along_rows(section)
    section = contract("fskbx,tsyk->ftbxy", arrived, backward)
    arrived = along_cols(section)
    return contract("fskab,szk->fabz", arrived, real_back)


def forward_pencil(physical, forward, real_fwd, along_cols, along_rows):
    section = contract("fabz,tkz->ftabk", physical, real_fwd)
    arrived = along_cols(section)
    section = contract("fsaqk,tspq->ftkap", arrived, forward)
    arrived = along_rows(section)
    return contract("fskqb,tspq->ftbkp", arrived, forward)


def wavenumber(indices, length):
    return jnp.where(indices < length // 2, indices, indices - length).astype(jnp.float32)


def shards(adjoint_hat, velocity, vorticity):
    length = adjoint_hat.shape[-1]
    backward, forward, real_back, real_fwd = tables(length)
    spectra = adjoint_hat[0]
    adjoint = inverse_pencil(
        spectra,
        backward,
        real_back,
        lambda block: lax.all_to_all(block, "row", split_axis=4, concat_axis=2, tiled=True),
        lambda block: lax.all_to_all(block, "col", split_axis=4, concat_axis=2, tiled=True),
    )
    wind_field = velocity[0]
    spin_field = vorticity[0]
    norm_factor = 1.0 / math.sqrt(lax.axis_size("env") * length**3)
    features = jnp.concatenate((wind_field, spin_field), 0)
    local_grad = (
        jnp.einsum("cabz,jabz->cj", adjoint, features, precision=HIGHEST_PRECISION) * norm_factor
    )
    controller_grad = lax.psum(local_grad, ("env", "row", "col"))
    crossed = jnp.stack(
        (
            spin_field[1] * adjoint[2] - spin_field[2] * adjoint[1],
            spin_field[2] * adjoint[0] - spin_field[0] * adjoint[2],
            spin_field[0] * adjoint[1] - spin_field[1] * adjoint[0],
        )
    )
    pieces = [
        forward_pencil(
            crossed[component : component + 1],
            forward,
            real_fwd,
            lambda block: lax.all_to_all(block, "col", split_axis=4, concat_axis=3, tiled=True),
            lambda block: lax.all_to_all(block, "row", split_axis=4, concat_axis=3, tiled=True),
        )
        for component in range(3)
    ]
    spectra_out = jnp.concatenate(pieces, 0)
    rows_local = spectra_out.shape[2]
    cols_local = spectra_out.shape[3]
    wave_y = wavenumber(
        lax.axis_index("row") * rows_local + lax.iota(jnp.int32, rows_local), length
    )[:, None, None]
    wave_z = wavenumber(
        lax.axis_index("col") * cols_local + lax.iota(jnp.int32, cols_local), length
    )[None, :, None]
    wave_x = wavenumber(lax.iota(jnp.int32, length), length)[None, None, :]
    kept_mask = (
        (3.0 * jnp.abs(wave_x) < length)
        & (3.0 * jnp.abs(wave_y) < length)
        & (3.0 * jnp.abs(wave_z) < length)
    ).astype(jnp.float32)
    wave_square = jnp.maximum(wave_x * wave_x + wave_y * wave_y + wave_z * wave_z, 1.0)
    inner = (
        wave_x * spectra_out[0] + wave_y * spectra_out[1] + wave_z * spectra_out[2]
    ) / wave_square
    adjoint_out = jnp.stack(
        (
            (spectra_out[0] - wave_x * inner) * kept_mask,
            (spectra_out[1] - wave_y * inner) * kept_mask,
            (spectra_out[2] - wave_z * inner) * kept_mask,
        )
    )[None]
    return (adjoint_out, controller_grad)


def solution(mesh):
    placed = (
        P("env", None, None, "row", "col", None),
        P("env", None, "row", "col", None),
        P("env", None, "row", "col", None),
    )
    return jax.shard_map(
        shards,
        mesh=mesh,
        in_specs=placed,
        out_specs=(P("env", None, None, "row", "col", None), P()),
        check_vma=False,
    )
```

profile of v0, /device:TPU:1, one launch (start us, length us, event | category | flops | bytes accessed | tf_op | source)
XLA Modules:
  0.0 671.6 jit_solution(6744752592070848433)
XLA Ops:
  2.9 8.1 %fusion.8 = f32[3,2,32,16,256]{4,2,3,0,1:T(8,128)} fusion(f32[3,2,32,16,256]{4,3,2,1,0:T(8,128)S(1)} %bitcast.266, f32[1,2,256,256]{3,2,1,0:T(8,128)S(1)} %get-tuple-element.16, f32[1,2,256,256]{3,2,1,0:T(8,128)S(1)} %get-tuple-element.19), kind=kOutput, calls=%fused_computation.15 | convolution fusion | flops 4832100352 | bytes 7340032 | tf_op jit(solution)/shard_map/fsabk,tsxk->ftabx/dot_general | solution.py:26
  11.0 11.5 %copy.46 = f32[3,2,32,16,256]{2,3,0,1,4:T(8,128)} copy(f32[3,2,32,16,256]{4,2,3,0,1:T(8,128)} %fusion.8) | data formatting | bytes 6291456 | tf_op jit(solution)/shard_map/fsabk,tsxk->ftabx/transpose | solution.py:26
  22.5 10.6 %reshape.324 = f32[8,1,98304]{2,1,0:T(1,128)} reshape(f32[256,2,3,16,32]{4,3,2,1,0:T(8,128)} %bitcast.243) | data formatting | bytes 6291456
  33.1 45.5 %all_to_all.126 = f32[8,1,98304]{2,1,0:T(1,128)} all-to-all(f32[8,1,98304]{2,1,0:T(1,128)} %reshape.324), channel_id=1, replica_groups=mesh['env'=2,'row'=8,'col'=16] {'row'}, dimensions={0} | all-to-all | bytes 6291456 | tf_op jit(solution)/shard_map/all_to_all | solution.py:57
  79.1 11.7 %reduce = f32[8,98304]{1,0:T(8,128)} reduce(f32[8,1,98304]{2,1,0:T(1,128)} %all_to_all.126, f32[]{:T(128)} %broadcast.386), dimensions={1}, to_apply=%all_to_all.92.reduce_sub_computation | reduce | bytes 6291460 | tf_op jit(solution)/shard_map/all_to_all | solution.py:57
  90.8 10.7 %reshape.325 = f32[256,2,3,16,32]{4,3,2,1,0:T(8,128)} reshape(f32[8,98304]{1,0:T(8,128)} %reduce) | data formatting | bytes 6291456
  101.5 16.3 %copy.122 = f32[3,2,32,16,8,32]{2,4,5,1,3,0:T(8,128)} copy(f32[3,2,32,16,8,32]{2,3,0,1,5,4:T(8,128)} %bitcast.239) | data formatting | bytes 6291456 | tf_op jit(solution)/shard_map/all_to_all | solution.py:57
  117.8 9.6 %reshape.298 = f32[3,2,256,16,32,1]{2,4,1,3,0,5:T(8,128)} reshape(f32[3,2,8,32,16,32]{3,2,5,1,4,0:T(8,128)} %bitcast.240) | data formatting | bytes 6291456 | tf_op jit(solution)/shard_map/all_to_all | solution.py:57
  127.5 7.9 %convolution_bitcast_fusion = f32[3,2,16,32,256]{4,3,2,0,1:T(8,128)} fusion(f32[3,2,256,16,32,1]{2,4,1,3,0,5:T(8,128)} %reshape.298, f32[1,2,256,256]{3,2,1,0:T(8,128)S(1)} %get-tuple-element.16, f32[1,2,256,256]{3,2,1,0:T(8,128)S(1)} %get-tuple-element.19), kind=kOutput, calls=%fused_computation.16 | convolution fusion | flops 4832100352 | bytes 7340032 | tf_op jit(solution)/shard_map/fskbx,tsyk->ftbxy/dot_general | solution.py:26
  135.4 11.7 %copy.48 = f32[3,2,16,32,256]{3,2,0,1,4:T(8,128)} copy(f32[3,2,16,32,256]{4,3,2,0,1:T(8,128)} %convolution_bitcast_fusion) | data formatting | bytes 6291456 | tf_op jit(solution)/shard_map/fskbx,tsyk->ftbxy/transpose | solution.py:26
  147.1 14.1 %reshape.326 = f32[16,1,49152]{2,1,0:T(1,128)} reshape(f32[256,2,3,16,32]{4,3,2,1,0:T(8,128)} %bitcast.244) | data formatting | bytes 6291456
  161.2 82.7 %all_to_all.127 = f32[16,1,49152]{2,1,0:T(1,128)} all-to-all(f32[16,1,49152]{2,1,0:T(1,128)} %reshape.326), channel_id=1, replica_groups=mesh['env'=2,'row'=8,'col'=16] {'col'}, dimensions={0} | all-to-all | bytes 6291456 | tf_op jit(solution)/shard_map/all_to_all | solution.py:58
  243.9 11.8 %reduce.1 = f32[16,49152]{1,0:T(8,128)} reduce(f32[16,1,49152]{2,1,0:T(1,128)} %all_to_all.127, f32[]{:T(128)} %broadcast.386), dimensions={1}, to_apply=%all_to_all.96.reduce_sub_computation | reduce | bytes 6291460 | tf_op jit(solution)/shard_map/all_to_all | solution.py:58
  255.7 12.6 %reshape.327 = f32[256,2,3,16,32]{4,3,2,1,0:T(8,128)} reshape(f32[16,49152]{1,0:T(8,128)} %reduce.1) | data formatting | bytes 6291456
  268.3 16.3 %copy.50 = f32[3,2,16,16,32,16]{4,5,3,2,1,0:T(8,128)} copy(f32[3,2,16,16,32,16]{4,3,0,1,5,2:T(8,128)} %bitcast.241) | data formatting | bytes 6291456 | tf_op jit(solution)/shard_map/all_to_all | solution.py:58
  284.6 11.0 %copy.51 = f32[3,2,256,32,16]{2,4,1,3,0:T(8,128)} copy(f32[3,2,256,32,16]{3,4,2,1,0:T(8,128)} %bitcast.242) | data formatting | bytes 6291456 | tf_op jit(solution)/shard_map/all_to_all | solution.py:58
  331.9 12.6 %all-to-all-done.6 = f32[16,1,16384]{2,1,0:T(1,128)} async-done(((f32[16,1,16384]{2,1,0:T(1,128)}), f32[16,1,16384]{2,1,0:T(1,128)}, u32[]{:S(2)}, u32[]{:S(2)}) %all-to-all-start.6) | async-done | bytes 1048608 | tf_op jit(solution)/shard_map/all_to_all | solution.py:80
  344.5 7.3 %all-to-all-start.4 = ((f32[16,1,16384]{2,1,0:T(1,128)}), f32[16,1,16384]{2,1,0:T(1,128)}, u32[]{:S(2)}, u32[]{:S(2)}) async-start(f32[16,1,16384]{2,1,0:T(1,128)} %reshape.332), calls=%async_computation.4 | async-start | bytes 2097152 | tf_op jit(solution)/shard_map/all_to_all | solution.py:80
  365.2 13.3 %all-to-all-done.4 = f32[16,1,16384]{2,1,0:T(1,128)} async-done(((f32[16,1,16384]{2,1,0:T(1,128)}), f32[16,1,16384]{2,1,0:T(1,128)}, u32[]{:S(2)}, u32[]{:S(2)}) %all-to-all-start.4) | async-done | bytes 1048608 | tf_op jit(solution)/shard_map/all_to_all | solution.py:80
  378.5 6.8 %all-to-all-start.2 = ((f32[16,1,16384]{2,1,0:T(1,128)}), f32[16,1,16384]{2,1,0:T(1,128)}, u32[]{:S(2)}, u32[]{:S(2)}) async-start(f32[16,1,16384]{2,1,0:T(1,128)} %reshape.336), calls=%async_computation.2 | async-start | bytes 2097152 | tf_op jit(solution)/shard_map/all_to_all | solution.py:80
  467.1 6.8 %copy_bitcast_fusion.4 = (f32[3,32,16,256]{3,0,2,1:T(4,128)}, f32[3,32,16,256]{3,0,2,1:T(4,128)}) fusion(f32[1,3,32,16,256]{4,3,2,1,0:T(8,128)} %param.5, f32[1,3,32,16,256]{4,3,2,1,0:T(8,128)} %param.4), kind=kLoop, calls=%fused_computation.13 | loop fusion | bytes 6291456 | tf_op jit(solution)/shard_map/squeeze | solution.py:61
  512.9 11.3 %fusion.16 = f32[3,6]{1,0:T(4,128)S(1)} fusion(f32[3,32,16,256]{3,0,2,1:T(4,128)} %get-tuple-element.23, f32[3,32,16,256]{3,0,2,1:T(4,128)} %get-tuple-element.24, f32[3,32,16,256]{3,2,1,0:T(8,128)S(1)} %convolution_bitcast_fusion.1), kind=kOutput, calls=%fused_computation.28 | convolution fusion | flops 29098002 | bytes 4718664 | tf_op jit(solution)/shard_map/cabz,jabz->cj/dot_general | solution.py:65
  524.2 77.9 %psum.7 = f32[3,6]{1,0:T(4,128)} all-reduce(f32[3,6]{1,0:T(4,128)S(1)} %fusion.16), channel_id=1, replica_groups=mesh['env'=2,'row'=8,'col'=16] {'env','row','col'}, use_global_device_ids=true, to_apply=%region_0.1 | all-reduce | flops 18 | bytes 144 | tf_op jit(solution)/shard_map/psum | solution.py:67
  627.8 6.6 copy.124
  (85 shorter events, 235.5 us)
Async XLA Ops:
  0.6 2.2 copy-start.3
  295.7 4.7 copy-start.1
  314.0 30.5 %all-to-all-start.6 = ((f32[16,1,16384]{2,1,0:T(1,128)}), f32[16,1,16384]{2,1,0:T(1,128)}, u32[]{:S(2)}, u32[]{:S(2)}) async-start(f32[16,1,16384]{2,1,0:T(1,128)} %reshape.328), calls=%async_computation.6 | async-start | bytes 2097152 | tf_op jit(solution)/shard_map/all_to_all | solution.py:80
  344.5 34.0 %all-to-all-start.4 = ((f32[16,1,16384]{2,1,0:T(1,128)}), f32[16,1,16384]{2,1,0:T(1,128)}, u32[]{:S(2)}, u32[]{:S(2)}) async-start(f32[16,1,16384]{2,1,0:T(1,128)} %reshape.332), calls=%async_computation.4 | async-start | bytes 2097152 | tf_op jit(solution)/shard_map/all_to_all | solution.py:80
  378.5 41.0 %all-to-all-start.2 = ((f32[16,1,16384]{2,1,0:T(1,128)}), f32[16,1,16384]{2,1,0:T(1,128)}, u32[]{:S(2)}, u32[]{:S(2)}) async-start(f32[16,1,16384]{2,1,0:T(1,128)} %reshape.336), calls=%async_computation.2 | async-start | bytes 2097152 | tf_op jit(solution)/shard_map/all_to_all | solution.py:80
  419.5 41.6 %all-to-all-start.7 = ((f32[8,1,32768]{2,1,0:T(1,128)}), f32[8,1,32768]{2,1,0:T(1,128)}, u32[]{:S(2)}, u32[]{:S(2)}) async-start(f32[8,1,32768]{2,1,0:T(1,128)} %reshape.330), calls=%async_computation.7 | async-start | bytes 2097152 | tf_op jit(solution)/shard_map/all_to_all | solution.py:81
  461.1 47.0 %all-to-all-start.5 = ((f32[8,1,32768]{2,1,0:T(1,128)}), f32[8,1,32768]{2,1,0:T(1,128)}, u32[]{:S(2)}, u32[]{:S(2)}) async-start(f32[8,1,32768]{2,1,0:T(1,128)} %reshape.334), calls=%async_computation.5 | async-start | bytes 2097152 | tf_op jit(solution)/shard_map/all_to_all | solution.py:81
  508.1 134.4 %all-to-all-start.3 = ((f32[8,1,32768]{2,1,0:T(1,128)}), f32[8,1,32768]{2,1,0:T(1,128)}, u32[]{:S(2)}, u32[]{:S(2)}) async-start(f32[8,1,32768]{2,1,0:T(1,128)} %reshape.338), calls=%async_computation.3 | async-start | bytes 2097152 | tf_op jit(solution)/shard_map/all_to_all | solution.py:81
  638.8 1.9 copy-start.2
  663.3 3.7 copy-start
where the time goes:
time: 682 us; the launch traced here: 672 us
  local copies, waits for them, and re-layouts  283 us (41%)
  blocking collectives  206 us (30%)
  matrix products  60.5 us (9%)
  other arithmetic  60 us (9%)
  starting transfers between devices  35 us (5%)
  waiting for transfers between devices  26 us (4%)
    unnamed x25, local copies, waits for them, and re-layouts  103 us
    all_to_all x1, blocking collectives, shards(): lax.all_to_all(block, 'col', split_axis=4, concat_axis=2, tiled=True)  82.7 us
    psum x1, blocking collectives, shards(): controller_grad = lax.psum(local_grad, ('env', 'row', 'col'))  77.9 us
    transpose x8, local copies, waits for them, and re-layouts, contract(): return jnp.einsum(pattern, values, table, precision=HIGHEST_PRECISION)  55.3 us
    dot_general x12, matrix products, contract(): return jnp.einsum(pattern, values, table, precision=HIGHEST_PRECISION)  49.2 us
    all_to_all x1, blocking collectives, shards(): lax.all_to_all(block, 'row', split_axis=4, concat_axis=2, tiled=True)  45.5 us
    all_to_all x2, local copies, waits for them, and re-layouts, shards(): lax.all_to_all(block, 'col', split_axis=4, concat_axis=2, tiled=True)  27.3 us
    all_to_all x3, local copies, waits for them, and re-layouts, shards(): lax.all_to_all(block, 'row', split_axis=4, concat_axis=2, tiled=True)  26.5 us
  transfers between devices with their start and end apart: 6, of which 2 were waited for; matrix products, arithmetic and copies ran while one was open for 28% of the time, Pallas kernels for 0%

commit v1 on v0

v1 whole, which is shorter than its diff:
```python
import math

import jax
import jax.numpy as jnp
import ml_dtypes
import numpy as np
from jax import lax
from jax.experimental import pallas as pl
from jax.experimental.pallas import tpu as pltpu
from jax.sharding import PartitionSpec as P

F32 = jnp.float32
BF16 = jnp.bfloat16
MESH = pl.DeviceIdType.MESH

N = 256
ROWS = 8
COLS = 16
KYS = 32
KZS = 16
PARTS = 4
ACTIVE_COLS = (0, 1, 2, 3, 4, 5, 10, 11, 12, 13, 14, 15)
ACTIVE_ROWS = (0, 1, 2, 5, 6, 7)
NCOL = len(ACTIVE_COLS)
NROW = len(ACTIVE_ROWS)


def halves(table):
    high = table.astype(np.float32).astype(ml_dtypes.bfloat16)
    low = (table - high.astype(np.float64)).astype(np.float32).astype(ml_dtypes.bfloat16)
    return high, low


def stacked(table, axis):
    high, low = halves(table)
    return np.concatenate((high, low, high), axis)


def wave(out_index, in_index):
    angles = (np.outer(out_index, in_index) % N) * (2.0 * math.pi / N)
    return np.cos(angles) / math.sqrt(N), np.sin(angles) / math.sqrt(N)


def x_order():
    order = np.zeros((2, 8, 16), np.int64)
    for half in range(2):
        for inner in range(8):
            for slot in range(16):
                order[half, inner, slot] = 32 * (slot & 7) + 8 * (2 * half + (slot >> 3)) + inner
    return order.reshape(2, 128)


def tables():
    every = np.arange(N)
    order = x_order()
    table_a = []
    for half in range(2):
        cosines, sines = wave(every, order[half])
        block = np.block([[cosines, sines], [-sines, cosines]])
        table_a.append(stacked(block, 0))
    table_a = np.stack(table_a)
    cosines, sines = wave(every, every)
    table_b = stacked(np.block([[cosines, -sines], [sines, cosines]]), 1)
    table_c = stacked(np.concatenate((cosines, -sines), 0), 0)
    pieces = []
    for col in ACTIVE_COLS:
        kept = slice(KZS * col, KZS * col + KZS)
        pieces += [cosines[:, kept], -sines[:, kept]]
    table_z = stacked(np.concatenate(pieces, 1), 0)
    pieces = []
    for row in ACTIVE_ROWS:
        kept = slice(KYS * row, KYS * row + KYS)
        pieces.append(np.concatenate((cosines[kept], sines[kept]), 1))
        pieces.append(np.concatenate((-sines[kept], cosines[kept]), 1))
    table_d = stacked(np.concatenate(pieces, 0), 1)
    cosines, sines = wave(order.reshape(-1), every)
    table_e = stacked(np.block([[cosines, -sines], [sines, cosines]]), 0)
    return table_a, table_b, table_c, table_z, table_d, table_e


def exchange(values, lane_bits):
    values = list(values)
    lane = lax.broadcasted_iota(jnp.int32, values[0].shape, 1)
    bit = 1
    while bit < len(values):
        step = bit * lane_bits
        clear = (lane & step) == 0
        for low in range(len(values)):
            if low & bit:
                continue
            first, second = values[low], values[low | bit]
            values[low] = jnp.where(clear, first, pltpu.roll(second, step, 1))
            values[low | bit] = jnp.where(clear, pltpu.roll(first, 128 - step, 1), second)
        bit *= 2
    return values


def split(value):
    high = value.astype(BF16)
    low = (value - high.astype(F32)).astype(BF16)
    return high, low


def matmul(left, right):
    return jnp.dot(left, right, preferred_element_type=F32)


def active_col(slot):
    return jnp.where(slot < 6, slot, slot + 4)


def active_row(slot):
    return jnp.where(slot < 3, slot, slot + 2)


def body(
    g_hbm, vel_hbm, vort_hbm, ta_hbm, tb_hbm, tc_hbm, tz_hbm, td_hbm,
    arrived, grad_out,
    g, feat, ta, tb, tc, tz, td,
    lhs_a, work_a, send_a, recv_a, rhs, send_b, recv_b,
    lhs_c, work_c, lhs_z, work_z, send_c, recv_c, send_d,
    grad_acc, grad_part, grad_row, grad_sum_row, grad_col, grad_sum_col, grad_env,
    load_sem, ra_sem, rb_sem, rc_sem, rd_sem, sa_sem, sb_sem, sc_sem, sd_sem,
    grad_recv, grad_send,
):
    env = lax.axis_index("env")
    row = lax.axis_index("row")
    col = lax.axis_index("col")
    col_active = (col < 6) | (col >= 10)
    row_active = (row < 3) | (row >= 5)

    loads = [pltpu.make_async_copy(ta_hbm, ta, load_sem.at[0])]
    for c in range(3):
        loads.append(pltpu.make_async_copy(g_hbm.at[c], g.at[c], load_sem.at[1 + c]))
    loads.append(pltpu.make_async_copy(tb_hbm, tb, load_sem.at[4]))
    loads.append(pltpu.make_async_copy(tc_hbm, tc, load_sem.at[5]))
    loads.append(pltpu.make_async_copy(vel_hbm, feat.at[pl.ds(0, 3)], load_sem.at[6]))
    loads.append(pltpu.make_async_copy(vort_hbm, feat.at[pl.ds(3, 3)], load_sem.at[7]))
    loads.append(pltpu.make_async_copy(tz_hbm, tz, load_sem.at[8]))
    loads.append(pltpu.make_async_copy(td_hbm, td, load_sem.at[9]))
    for load in loads:
        load.start()

    barrier = pltpu.get_barrier_semaphore()

    def greet_row(k, _):
        pl.semaphore_signal(
            barrier, inc=1, device_id={"row": lax.rem(row + k, ROWS)}, device_id_type=MESH
        )
        return 0

    def greet_col(k, _):
        pl.semaphore_signal(
            barrier, inc=1, device_id={"col": lax.rem(col + k, COLS)}, device_id_type=MESH
        )
        return 0

    lax.fori_loop(1, ROWS, greet_row, 0)
    lax.fori_loop(1, COLS, greet_col, 0)
    pl.semaphore_signal(barrier, inc=1, device_id={"env": 1 - env}, device_id_type=MESH)

    def spectrum_x(half, c):
        out = matmul(lhs_a[c], ta[half])
        work_a[0] = out[:, :128]
        work_a[1] = out[:, 128:]

        def pack(step, _):
            t = step // 4
            tile = step % 4
            values = [
                work_a[t, pl.ds(tile * 128 + kz, 8, stride=16), :] for kz in range(16)
            ]
            values = exchange(values, 1)
            for slot in range(16):
                send_a[2 * half + (slot >> 3), slot & 7, c, t, pl.ds(tile * 8, 8), :] = values[slot]
            return 0

        lax.fori_loop(0, 8, pack, 0)

    def start_row(j):
        def one(k, _):
            to = lax.rem(row + k, ROWS)
            pltpu.make_async_remote_copy(
                src_ref=send_a.at[j, to],
                dst_ref=recv_a.at[j, :, :, pl.ds(KYS * row, KYS), :],
                send_sem=sa_sem,
                recv_sem=ra_sem.at[j],
                device_id={"row": to},
                device_id_type=MESH,
            ).start()
            return 0

        lax.fori_loop(1, ROWS, one, 0)
        pltpu.make_async_copy(
            send_a.at[j, row], recv_a.at[j, :, :, pl.ds(KYS * row, KYS), :], ra_sem.at[j]
        ).start()

    loads[0].wait()
    for half in range(2):
        for c in range(3):
            if half == 0:
                loads[1 + c].wait()
                for s in range(2):
                    high, low = split(g[c, s])
                    lhs_a[c, :, 256 * s : 256 * s + 256] = high
                    lhs_a[c, :, 512 + 256 * s : 768 + 256 * s] = high
                    lhs_a[c, :, 1024 + 256 * s : 1280 + 256 * s] = low
            spectrum_x(half, c)
        if half == 0:
            pl.semaphore_wait(barrier, ROWS - 1 + COLS - 1 + 1)
        start_row(2 * half)
        start_row(2 * half + 1)

    loads[4].wait()

    def stage_b(j, _):
        pltpu.make_async_copy(recv_a.at[j], recv_a.at[j], ra_sem.at[j]).wait()
        for c in range(3):
            for s in range(2):
                high, low = split(recv_a[j, c, s])
                rhs[256 * s : 256 * s + 256, 128 * c : 128 * c + 128] = high
                rhs[512 + 256 * s : 768 + 256 * s, 128 * c : 128 * c + 128] = high
                rhs[1024 + 256 * s : 1280 + 256 * s, 128 * c : 128 * c + 128] = low
        out = matmul(tb[...], rhs[...])
        for c in range(3):
            for t in range(2):
                send_b[j, c, t] = out[256 * t : 256 * t + 256, 128 * c : 128 * c + 128]

        def one(k, _):
            to = lax.rem(col + k, COLS)
            pltpu.make_async_remote_copy(
                src_ref=send_b.at[j, :, :, pl.ds(KZS * to, KZS), :],
                dst_ref=recv_b.at[j, col],
                send_sem=sb_sem,
                recv_sem=rb_sem.at[j],
                device_id={"col": to},
                device_id_type=MESH,
            ).start()
            return 0

        lax.fori_loop(1, COLS, one, 0)
        pltpu.make_async_copy(
            send_b.at[j, :, :, pl.ds(KZS * col, KZS), :], recv_b.at[j, col], rb_sem.at[j]
        ).start()
        return 0

    lax.fori_loop(0, PARTS, stage_b, 0)

    for load in loads[5:9]:
        load.wait()
    grad_acc[...] = jnp.zeros_like(grad_acc)

    def stage_c(j, _):
        pltpu.make_async_copy(recv_b.at[j], recv_b.at[j], rb_sem.at[j]).wait()

        def gather(step, _):
            c = step // 2
            s = step % 2
            for group in range(2):
                values = [recv_b[j, 8 * group + k, c, s] for k in range(8)]
                values = exchange(values, 16)
                for x in range(8):
                    high, low = split(values[x])
                    rows = pl.ds(pl.multiple_of(128 * c + 16 * x, 16), 16)
                    at = pl.multiple_of(256 * s + 128 * group, 128)
                    lhs_c[rows, pl.ds(at, 128)] = high
                    lhs_c[rows, pl.ds(at + 512, 128)] = high
                    lhs_c[rows, pl.ds(at + 1024, 128)] = low
            return 0

        lax.fori_loop(0, 6, gather, 0)
        work_c[...] = matmul(lhs_c[...], tc[...])

        def cross(i, _):
            here = pl.ds(pl.multiple_of(16 * i, 16), 16)
            there = pl.ds(pl.multiple_of(128 * j + 16 * i, 16), 16)
            adjoint = [work_c[pl.ds(pl.multiple_of(128 * c + 16 * i, 16), 16), :] for c in range(3)]
            for f in range(6):
                feature = feat[f, there, :]
                for c in range(3):
                    product = adjoint[c] * feature
                    total = (product[:8, :128] + product[:8, 128:]) + (
                        product[8:, :128] + product[8:, 128:]
                    )
                    grad_acc[6 * c + f] += total
            spin = [feat[3 + c, there, :] for c in range(3)]
            for c in range(3):
                second, third = (c + 1) % 3, (c + 2) % 3
                high, low = split(
                    spin[second] * adjoint[third] - spin[third] * adjoint[second]
                )
                rows = pl.ds(pl.multiple_of(128 * c + 16 * i, 16), 16)
                lhs_z[rows, 0:256] = high
                lhs_z[rows, 256:512] = high
                lhs_z[rows, 512:768] = low
            return 0

        lax.fori_loop(0, 8, cross, 0)
        work_z[...] = matmul(lhs_z[...], tz[...])

        def scatter(c, _):
            for n in range(3):
                values = [
                    work_z[
                        pl.ds(pl.multiple_of(128 * c + 16 * x, 16), 16), 128 * n : 128 * n + 128
                    ]
                    for x in range(8)
                ]
                values = exchange(values, 16)
                for b in range(8):
                    block = 8 * n + b
                    send_c[j, block >> 1, block & 1, c] = values[b]
            return 0

        lax.fori_loop(0, 3, scatter, 0)

        def one(slot, _):
            to = active_col(slot)
            mine = recv_c.at[j, :, :, pl.ds(KZS * col, KZS), :]

            @pl.when(to != col)
            def _():
                pltpu.make_async_remote_copy(
                    src_ref=send_c.at[j, slot],
                    dst_ref=mine,
                    send_sem=sc_sem,
                    recv_sem=rc_sem.at[j],
                    device_id={"col": to},
                    device_id_type=MESH,
                ).start()

            @pl.when(to == col)
            def _():
                pltpu.make_async_copy(send_c.at[j, slot], mine, rc_sem.at[j]).start()

            return 0

        lax.fori_loop(0, NCOL, one, 0)
        return 0

    lax.fori_loop(0, PARTS, stage_c, 0)

    for k in range(18):
        grad_part[k : k + 1, :] = jnp.sum(grad_acc[k], axis=0, keepdims=True)
    grad_part[18:24, :] = jnp.zeros((6, 128), F32)

    def share_row(k, _):
        pltpu.make_async_remote_copy(
            src_ref=grad_part,
            dst_ref=grad_row.at[row],
            send_sem=grad_send.at[0],
            recv_sem=grad_recv.at[0],
            device_id={"row": lax.rem(row + k, ROWS)},
            device_id_type=MESH,
        ).start()
        return 0

    lax.fori_loop(1, ROWS, share_row, 0)
    pltpu.make_async_copy(grad_part, grad_row.at[row], grad_recv.at[0]).start()

    loads[9].wait()

    def stage_d(j, _):
        @pl.when(col_active)
        def _():
            pltpu.make_async_copy(recv_c.at[j], recv_c.at[j], rc_sem.at[j]).wait()
            for c in range(3):
                for s in range(2):
                    high, low = split(recv_c[j, s, c])
                    rhs[256 * s : 256 * s + 256, 128 * c : 128 * c + 128] = high
                    rhs[512 + 256 * s : 768 + 256 * s, 128 * c : 128 * c + 128] = high
                    rhs[1024 + 256 * s : 1280 + 256 * s, 128 * c : 128 * c + 128] = low
            out = matmul(td[...], rhs[...])
            for slot in range(NROW):
                for t in range(2):
                    for c in range(3):
                        at = 64 * slot + 32 * t
                        send_d[j, slot, t, c] = out[at : at + 32, 128 * c : 128 * c + 128]

            def one(slot, _):
                to = active_row(slot)

                @pl.when(to != row)
                def _():
                    pltpu.make_async_remote_copy(
                        src_ref=send_d.at[j, slot],
                        dst_ref=arrived.at[row, j],
                        send_sem=sd_sem,
                        recv_sem=rd_sem,
                        device_id={"row": to},
                        device_id_type=MESH,
                    ).start()

                @pl.when(to == row)
                def _():
                    pltpu.make_async_copy(send_d.at[j, slot], arrived.at[row, j], rd_sem).start()

                return 0

            lax.fori_loop(0, NROW, one, 0)

        return 0

    lax.fori_loop(0, 2, stage_d, 0)

    pltpu.make_async_copy(grad_row, grad_row, grad_recv.at[0]).wait()
    grad_sum_row[...] = jnp.sum(grad_row[...], axis=0)

    def share_col(k, _):
        pltpu.make_async_remote_copy(
            src_ref=grad_sum_row,
            dst_ref=grad_col.at[col],
            send_sem=grad_send.at[1],
            recv_sem=grad_recv.at[1],
            device_id={"col": lax.rem(col + k, COLS)},
            device_id_type=MESH,
        ).start()
        return 0

    lax.fori_loop(1, COLS, share_col, 0)
    pltpu.make_async_copy(grad_sum_row, grad_col.at[col], grad_recv.at[1]).start()

    lax.fori_loop(2, 3, stage_d, 0)

    pltpu.make_async_copy(grad_col, grad_col, grad_recv.at[1]).wait()
    grad_sum_col[...] = jnp.sum(grad_col[...], axis=0)
    pltpu.make_async_remote_copy(
        src_ref=grad_sum_col,
        dst_ref=grad_env.at[env],
        send_sem=grad_send.at[2],
        recv_sem=grad_recv.at[2],
        device_id={"env": 1 - env},
        device_id_type=MESH,
    ).start()
    pltpu.make_async_copy(grad_sum_col, grad_env.at[env], grad_recv.at[2]).start()

    lax.fori_loop(3, 4, stage_d, 0)

    pltpu.make_async_copy(grad_env, grad_env, grad_recv.at[2]).wait()
    total = jnp.sum(grad_env[0] + grad_env[1], axis=1, keepdims=True)
    total = total * (1.0 / math.sqrt(2 * N**3))
    grad_out[...] = jnp.broadcast_to(total, (24, 128))

    for j in range(PARTS):
        sent_a = send_a.at[j, pl.ds(0, ROWS - 1)]
        pltpu.make_async_copy(sent_a, sent_a, sa_sem).wait()
        sent_b = recv_b.at[j, pl.ds(0, COLS - 1)]
        pltpu.make_async_copy(sent_b, sent_b, sb_sem).wait()

        @pl.when(col_active)
        def _():
            sent_c = send_c.at[j, pl.ds(0, NCOL - 1)]
            pltpu.make_async_copy(sent_c, sent_c, sc_sem).wait()

            @pl.when(row_active)
            def _():
                sent_d = send_d.at[j, pl.ds(0, NROW - 1)]
                pltpu.make_async_copy(sent_d, sent_d, sd_sem).wait()

            @pl.when(jnp.logical_not(row_active))
            def _():
                sent_d = send_d.at[j]
                pltpu.make_async_copy(sent_d, sent_d, sd_sem).wait()

        @pl.when(jnp.logical_not(col_active))
        def _():
            sent_c = send_c.at[j]
            pltpu.make_async_copy(sent_c, sent_c, sc_sem).wait()

    sent = grad_row.at[pl.ds(0, ROWS - 1)]
    pltpu.make_async_copy(sent, sent, grad_send.at[0]).wait()
    sent = grad_col.at[pl.ds(0, COLS - 1)]
    pltpu.make_async_copy(sent, sent, grad_send.at[1]).wait()
    sent = grad_env.at[0]
    pltpu.make_async_copy(sent, sent, grad_send.at[2]).wait()

    @pl.when(col_active & row_active)
    def _():
        pltpu.make_async_copy(arrived, arrived, rd_sem).wait()


def last_body(arrived, te, out, work, lhs, spec):
    row = lax.axis_index("row")
    col = lax.axis_index("col")
    tile = pl.program_id(0)
    active = ((col < 6) | (col >= 10)) & ((row < 3) | (row >= 5))

    @pl.when(jnp.logical_not(active))
    def _():
        out[...] = jnp.zeros_like(out)

    @pl.when(active)
    def _():
        def gather(step, _):
            c = step // 2
            s = step % 2
            for half in range(2):
                values = [arrived[slot & 7, 2 * half + (slot >> 3), s, c] for slot in range(16)]
                values = exchange(values, 1)
                at = pl.multiple_of(256 * s + 128 * half, 128)
                for kz in range(0, 16, 2):
                    high, low = split(jnp.concatenate((values[kz], values[kz + 1]), 0))
                    rows = pl.ds(pl.multiple_of(128 * c + 8 * kz, 16), 16)
                    lhs[rows, pl.ds(at, 128)] = high
                    lhs[rows, pl.ds(at + 512, 128)] = high
                    lhs[rows, pl.ds(at + 1024, 128)] = low
            return 0

        lax.fori_loop(0, 6, gather, 0)
        spec[...] = matmul(lhs[...], te[...])

        def signed(index):
            return jnp.where(index < N // 2, index, index - N).astype(F32)

        wave_x = signed(lax.broadcasted_iota(jnp.int32, (8, 256), 1))
        wave_y = signed(
            lax.broadcasted_iota(jnp.int32, (8, 256), 0) + (KYS * row + 8 * tile)
        )
        kept_xy = (3.0 * jnp.abs(wave_x) < N) & (3.0 * jnp.abs(wave_y) < N)
        square_xy = wave_x * wave_x + wave_y * wave_y

        def project(kz, _):
            wave_z = signed(jnp.full((8, 256), KZS * col + kz, jnp.int32))
            kept = kept_xy & (3.0 * jnp.abs(wave_z) < N)
            square = jnp.maximum(square_xy + wave_z * wave_z, 1.0)
            inverse = 1.0 / square
            waves = (wave_x, wave_y, wave_z)
            for t in range(2):
                parts = [
                    spec[
                        pl.ds(pl.multiple_of(128 * c + 8 * kz, 8), 8), 256 * t : 256 * t + 256
                    ]
                    for c in range(3)
                ]
                inner = (
                    wave_x * parts[0] + wave_y * parts[1] + wave_z * parts[2]
                ) * inverse
                for c in range(3):
                    value = jnp.where(kept, parts[c] - waves[c] * inner, 0.0)
                    for lanes in range(2):
                        work[c, t, lanes, pl.ds(kz, 8, stride=16), :] = value[
                            :, 128 * lanes : 128 * lanes + 128
                        ]
            return 0

        lax.fori_loop(0, 16, project, 0)
        for c in range(3):
            for t in range(2):
                for lanes in range(2):
                    out[c, t, :, 128 * lanes : 128 * lanes + 128] = work[c, t, lanes]


def shards(adjoint_hat, velocity, vorticity):
    table_a, table_b, table_c, table_z, table_d, table_e = (jnp.asarray(t) for t in tables())
    hbm = pl.BlockSpec(memory_space=pl.ANY)
    vmem = pltpu.VMEM
    dma = pltpu.SemaphoreType.DMA
    arrived, grad = pl.pallas_call(
        body,
        name="advect",
        out_shape=(
            jax.ShapeDtypeStruct((ROWS, PARTS, 2, 3, KYS, 128), F32),
            jax.ShapeDtypeStruct((24, 128), F32),
        ),
        in_specs=[hbm] * 8,
        out_specs=(hbm, pl.BlockSpec(memory_space=pltpu.VMEM)),
        scratch_shapes=[
            vmem((3, 2, 512, 256), F32),
            vmem((6, 512, 256), F32),
            vmem((2, 1536, 256), BF16),
            vmem((512, 1536), BF16),
            vmem((1536, 256), BF16),
            vmem((768, 384), BF16),
            vmem((384, 1536), BF16),
            vmem((3, 512, 1536), BF16),
            vmem((2, 512, 128), F32),
            vmem((PARTS, ROWS, 3, 2, KYS, 128), F32),
            vmem((PARTS, 3, 2, N, 128), F32),
            vmem((1536, 384), BF16),
            vmem((PARTS, 3, 2, N, 128), F32),
            vmem((PARTS, COLS, 3, 2, KZS, 128), F32),
            vmem((384, 1536), BF16),
            vmem((384, 256), F32),
            vmem((384, 768), BF16),
            vmem((384, 384), F32),
            vmem((PARTS, NCOL, 2, 3, KZS, 128), F32),
            vmem((PARTS, 2, 3, N, 128), F32),
            vmem((PARTS, NROW, 2, 3, KYS, 128), F32),
            vmem((18, 8, 128), F32),
            vmem((24, 128), F32),
            vmem((ROWS, 24, 128), F32),
            vmem((24, 128), F32),
            vmem((COLS, 24, 128), F32),
            vmem((24, 128), F32),
            vmem((2, 24, 128), F32),
            dma((10,)),
            dma((PARTS,)),
            dma((PARTS,)),
            dma((PARTS,)),
            dma,
            dma,
            dma,
            dma,
            dma,
            dma((3,)),
            dma((3,)),
        ],
        compiler_params=pltpu.CompilerParams(
            collective_id=0, has_side_effects=True, vmem_limit_bytes=60 * 2**20
        ),
    )(
        adjoint_hat.reshape(3, 2, 512, 256),
        velocity.reshape(3, 512, 256),
        vorticity.reshape(3, 512, 256),
        table_a, table_b, table_c, table_z, table_d,
    )
    out = pl.pallas_call(
        last_body,
        name="project",
        grid=(4,),
        out_shape=jax.ShapeDtypeStruct((3, 2, 512, 256), F32),
        in_specs=[
            pl.BlockSpec((ROWS, PARTS, 2, 3, 8, 128), lambda i: (0, 0, 0, 0, i, 0)),
            pl.BlockSpec((1536, 512), lambda i: (0, 0)),
        ],
        out_specs=pl.BlockSpec((3, 2, 128, 256), lambda i: (0, 0, i, 0)),
        scratch_shapes=[
            vmem((3, 2, 2, 128, 128), F32),
            vmem((384, 1536), BF16),
            vmem((384, 512), F32),
        ],
        compiler_params=pltpu.CompilerParams(vmem_limit_bytes=40 * 2**20),
    )(arrived, table_e)
    return out.reshape(adjoint_hat.shape), grad[:18, 0].reshape(3, 6)


def solution(mesh):
    placed = (
        P("env", None, None, "row", "col", None),
        P("env", None, "row", "col", None),
        P("env", None, "row", "col", None),
    )
    return jax.shard_map(
        shards,
        mesh=mesh,
        in_specs=placed,
        out_specs=(P("env", None, None, "row", "col", None), P()),
        check_vma=False,
    )
```

time: 682 us -> 207 us (0.30); the launches traced: 672 us -> 207 us
  local copies, waits for them, and re-layouts: 283 us -> 2.67 us
  blocking collectives: 206 us -> 0 us
  Pallas kernels: 0 us -> 203 us
  matrix products: 60.5 us -> 0 us
  other arithmetic: 60 us -> 0 us
  starting transfers between devices: 35 us -> 0 us
  waiting for transfers between devices: 26 us -> 0 us
    pallas_call x0 -> x2, Pallas kernels: none -> 203 us  [the longest x1 188 us: shards(): pl.pallas_call(body, name='advect', out_shape=(jax.ShapeDtypeStruct((ROWS...]
    all_to_all x2 -> x0, blocking collectives: 128 us -> none  [the longest x1 82.7 us: shards(): lax.all_to_all(block, 'col', split_axis=4, concat_axis=2, tiled=True)]
    unnamed x25 -> x6, local copies, waits for them, and re-layouts: 103 us -> 1.89 us
    all_to_all x14 -> x0, local copies, waits for them, and re-layouts: 94.9 us -> none  [the longest x2 27.3 us: shards(): lax.all_to_all(block, 'col', split_axis=4, concat_axis=2, tiled=True)]
    psum x1 -> x0, blocking collectives: 77.9 us -> none  [shards(): controller_grad = lax.psum(local_grad, ('env', 'row', 'col'))]
    dot_general x13 -> x0, matrix products: 60.5 us -> none  [the longest x12 49.2 us: contract(): return jnp.einsum(pattern, values, table, precision=HIGHEST_PRECISION)]
    transpose x8 -> x0, local copies, waits for them, and re-layouts: 55.3 us -> none  [contract(): return jnp.einsum(pattern, values, table, precision=HIGHEST_PRECISION)]
    all_to_all x8 -> x0, other arithmetic: 53.4 us -> none  [the longest x3 16 us: shards(): lax.all_to_all(block, 'col', split_axis=4, concat_axis=3, tiled=True)]
  transfers between devices with their start and end apart: 6 -> 0, of which waited for: 2 -> 0; matrix products, arithmetic and copies ran while one was open for 28% -> 0% of each run, Pallas kernels for 0% -> 0%
where the time goes in v1:
time: 207 us
  Pallas kernels  203 us (98%)
  local copies, waits for them, and re-layouts  2.67 us (1%)
    pallas_call x1, Pallas kernels, shards(): pl.pallas_call(body, name='advect', out_shape=(jax.ShapeDtypeStruct((ROWS...  188 us
    pallas_call x1, Pallas kernels, shards(): pl.pallas_call(last_body, name='project', grid=(4,), out_shape=jax.ShapeD...  15 us

profile of v1, /device:TPU:1, one launch (start us, length us, event | category | flops | bytes accessed | tf_op | source)
XLA Modules:
  0.0 206.7 jit_solution(9248577565478160963)
XLA Ops:
  0.6 0.0 copy-start.1
  0.6 188.4 %advect.1 = (f32[8,4,2,3,32,128]{5,4,3,2,1,0:T(8,128)}, f32[24,128]{1,0:T(8,128)}) custom-call(f32[3,2,512,256]{3,2,1,0:T(8,128)} %bitcast.4, f32[3,512,256]{2,1,0:T(8,128)} %bitcast.6, f32[3,512,256]{2,1,0:T(8,128)} %bitcast.7, bf16[2,1536,256]{2,1,0:T(8,128)(2,1)} %constant.12.clone.ta_hbm, bf16[512,1536]{1,0:T(8,128)(2,1)} %constant.13.clone.tb_hbm, ...), custom_call_target="tpu_custom_call" | custom-call | tf_op jit(solution)/shard_map/advect/pallas_call | solution.py:558
  189.0 0.0 copy-done.1
  189.0 0.0 copy-start
  189.0 1.9 copy-done
  190.9 0.0 copy-start.2
  190.9 15.0 %project.1 = f32[3,2,512,256]{3,2,1,0:T(8,128)} custom-call(f32[8,4,2,3,32,128]{5,4,3,2,1,0:T(8,128)S(1)} %copy-done, bf16[1536,512]{1,0:T(8,128)(2,1)S(1)} %copy-done.1), custom_call_target="tpu_custom_call" | custom-call | tf_op jit(solution)/shard_map/project/pallas_call | solution.py:617
  206.0 0.0 copy-done.2
  206.0 0.1 slice_reduce_fusion
  206.1 0.7 reshape_squeeze.3
Async XLA Ops:
  0.6 188.4 %copy-start.1 = (bf16[1536,512]{1,0:T(8,128)(2,1)S(1)}, bf16[1536,512]{1,0:T(8,128)(2,1)}, u32[]{:S(2)}) copy-start(bf16[1536,512]{1,0:T(8,128)(2,1)} %constant.17.clone.te) | copy-start | bytes 4718596
  189.0 1.9 copy-start
  190.9 15.0 %copy-start.2 = (f32[24,128]{1,0:T(8,128)S(1)}, f32[24,128]{1,0:T(8,128)}, u32[]{:S(2)}) copy-start(f32[24,128]{1,0:T(8,128)} %get-tuple-element.5) | copy-start | bytes 36868

commit v2 on v1

v2 whole, which is shorter than its diff:
```python
import math

import jax
import jax.numpy as jnp
import ml_dtypes
import numpy as np
from jax import lax
from jax.experimental import pallas as pl
from jax.experimental.pallas import tpu as pltpu
from jax.sharding import PartitionSpec as P

F32 = jnp.float32
BF16 = jnp.bfloat16
MESH = pl.DeviceIdType.MESH

N = 256
ROWS = 8
COLS = 16
KYS = 32
KZS = 16
PARTS = 4
ACTIVE_COLS = (0, 1, 2, 3, 4, 5, 10, 11, 12, 13, 14, 15)
ACTIVE_ROWS = (0, 1, 2, 5, 6, 7)
NCOL = len(ACTIVE_COLS)
NROW = len(ACTIVE_ROWS)


def halves(table):
    high = table.astype(np.float32).astype(ml_dtypes.bfloat16)
    low = (table - high.astype(np.float64)).astype(np.float32).astype(ml_dtypes.bfloat16)
    return high, low


def stacked(table, axis):
    high, low = halves(table)
    return np.concatenate((high, low, high), axis)


def wave(out_index, in_index):
    angles = (np.outer(out_index, in_index) % N) * (2.0 * math.pi / N)
    return np.cos(angles) / math.sqrt(N), np.sin(angles) / math.sqrt(N)


def x_order():
    order = np.zeros((PARTS, ROWS, 8), np.int64)
    for part in range(PARTS):
        for row in range(ROWS):
            order[part, row] = 32 * row + 8 * part + np.arange(8)
    return order


def tables():
    every = np.arange(N)
    order = x_order()
    pieces = []
    for part in range(PARTS):
        cosines, sines = wave(order[part].reshape(-1), every)
        pieces.append(np.block([[cosines, -sines], [sines, cosines]]))
    table_a = stacked(np.concatenate(pieces, 0), 1)
    cosines, sines = wave(every, every)
    table_b = stacked(np.block([[cosines, -sines], [sines, cosines]]), 1)
    kz_order = np.arange(N).reshape(2, 8, KZS).transpose(0, 2, 1).reshape(-1)
    table_c = stacked(np.concatenate((cosines[kz_order], -sines[kz_order]), 0), 0)
    pieces = []
    for col in ACTIVE_COLS:
        kept = slice(KZS * col, KZS * col + KZS)
        pieces += [cosines[:, kept], -sines[:, kept]]
    table_z = stacked(np.concatenate(pieces, 1), 0)
    pieces = []
    for row in ACTIVE_ROWS:
        kept = slice(KYS * row, KYS * row + KYS)
        pieces.append(np.concatenate((cosines[kept], sines[kept]), 1))
        pieces.append(np.concatenate((-sines[kept], cosines[kept]), 1))
    table_d = stacked(np.concatenate(pieces, 0), 1)
    table_e = []
    for part in range(PARTS):
        block = np.zeros((8, 2, ROWS, 2, N))
        for row in range(ROWS):
            cosines, sines = wave(order[part, row], every)
            block[:, 0, row, 0], block[:, 0, row, 1] = cosines, -sines
            block[:, 1, row, 0], block[:, 1, row, 1] = sines, cosines
        table_e.append(stacked(block.reshape(128, 2 * N), 0))
    return table_a, table_b, table_c, table_z, table_d, np.stack(table_e)


def exchange(values, lane_bits):
    values = list(values)
    lane = lax.broadcasted_iota(jnp.int32, values[0].shape, 1)
    bit = 1
    while bit < len(values):
        step = bit * lane_bits
        clear = (lane & step) == 0
        for low in range(len(values)):
            if low & bit:
                continue
            first, second = values[low], values[low | bit]
            values[low] = jnp.where(clear, first, pltpu.roll(second, step, 1))
            values[low | bit] = jnp.where(clear, pltpu.roll(first, 128 - step, 1), second)
        bit *= 2
    return values


def split(value):
    high = value.astype(BF16)
    low = (value - high.astype(F32)).astype(BF16)
    return high, low


def matmul(left, right):
    return jnp.dot(left, right, preferred_element_type=F32)


def matmul_t(left, right):
    return lax.dot_general(
        left, right, (((1,), (1,)), ((), ())), preferred_element_type=F32
    )


def active_col(slot):
    return jnp.where(slot < 6, slot, slot + 4)


def active_row(slot):
    return jnp.where(slot < 3, slot, slot + 2)


def body(
    g_hbm, vel_hbm, vort_hbm, ta_hbm, tb_hbm, tc_hbm, tz_hbm, td_hbm, te_hbm,
    spec_out, grad_out,
    g, feat, ta, tb, tc, tz, td, te,
    data_a, send_a, recv_a, data_b, send_b, recv_b,
    lhs_c, work_c, lhs_z, work_z, send_c, recv_c, rhs, send_d, recv_d, lhs_e, spec,
    grad_acc, grad_part, grad_row, grad_sum_row, grad_col, grad_sum_col, grad_env,
    load_sem, ra_sem, rb_sem, rc_sem, rd_sem, sa_sem, sb_sem, sc_sem, sd_sem,
    grad_recv, grad_send, out_sem,
):
    env = lax.axis_index("env")
    row = lax.axis_index("row")
    col = lax.axis_index("col")
    col_active = (col < 6) | (col >= 10)
    row_active = (row < 3) | (row >= 5)

    barrier = pltpu.get_barrier_semaphore()

    def greet_row(k, _):
        pl.semaphore_signal(
            barrier, inc=1, device_id={"row": lax.rem(row + k, ROWS)}, device_id_type=MESH
        )
        return 0

    def greet_col(k, _):
        pl.semaphore_signal(
            barrier, inc=1, device_id={"col": lax.rem(col + k, COLS)}, device_id_type=MESH
        )
        return 0

    lax.fori_loop(1, ROWS, greet_row, 0)
    lax.fori_loop(1, COLS, greet_col, 0)
    pl.semaphore_signal(barrier, inc=1, device_id={"env": 1 - env}, device_id_type=MESH)

    def load_g(c):
        def one(kz, _):
            for s in range(2):
                pltpu.make_async_copy(
                    g_hbm.at[c, s, :, kz, :], g.at[c, s, kz], load_sem.at[1 + c]
                ).start()
            return 0

        lax.fori_loop(0, KZS, one, 0)

    loads = [pltpu.make_async_copy(ta_hbm, ta, load_sem.at[0])]
    for c in range(3):
        loads.append(pltpu.make_async_copy(g.at[c], g.at[c], load_sem.at[1 + c]))
    loads.append(pltpu.make_async_copy(tb_hbm, tb, load_sem.at[4]))
    loads.append(pltpu.make_async_copy(tc_hbm, tc, load_sem.at[5]))
    loads.append(pltpu.make_async_copy(vel_hbm, feat.at[pl.ds(0, 3)], load_sem.at[6]))
    loads.append(pltpu.make_async_copy(vort_hbm, feat.at[pl.ds(3, 3)], load_sem.at[7]))
    loads.append(pltpu.make_async_copy(tz_hbm, tz, load_sem.at[8]))
    loads.append(pltpu.make_async_copy(td_hbm, td, load_sem.at[9]))
    loads.append(pltpu.make_async_copy(te_hbm, te, load_sem.at[10]))
    load_g(0)
    loads[0].start()
    load_g(1)
    load_g(2)
    for load in loads[4:]:
        load.start()

    def start_row(c, j):
        def one(k, _):
            to = lax.rem(row + k, ROWS)
            pltpu.make_async_remote_copy(
                src_ref=send_a.at[c, j, to],
                dst_ref=recv_a.at[c, j, row],
                send_sem=sa_sem,
                recv_sem=ra_sem.at[c, j],
                device_id={"row": to},
                device_id_type=MESH,
            ).start()
            return 0

        lax.fori_loop(1, ROWS, one, 0)
        pltpu.make_async_copy(send_a.at[c, j, row], recv_a.at[c, j, row], ra_sem.at[c, j]).start()

    for c in range(3):
        loads[1 + c].wait()
        for s in range(2):
            high, low = split(g[c, s].reshape(512, 256))
            data_a[:, 256 * s : 256 * s + 256] = high
            data_a[:, 512 + 256 * s : 768 + 256 * s] = high
            data_a[:, 1024 + 256 * s : 1280 + 256 * s] = low
        if c == 0:
            loads[0].wait()
        for half in range(2):
            out = matmul_t(ta[256 * half : 256 * half + 256, :], data_a[...])
            for part in range(2):
                for t in range(2):
                    for r in range(ROWS):
                        at = 128 * part + 64 * t + 8 * r
                        for m in range(4):
                            send_a[c, 2 * half + part, r, t, m] = out[
                                at : at + 8, 128 * m : 128 * m + 128
                            ]
            if c == 0 and half == 0:
                pl.semaphore_wait(barrier, ROWS - 1 + COLS - 1 + 1)
            start_row(c, 2 * half)
            start_row(c, 2 * half + 1)

    loads[4].wait()

    def stage_b(unit, _):
        c = unit // PARTS
        j = unit % PARTS
        pltpu.make_async_copy(recv_a.at[c, j], recv_a.at[c, j], ra_sem.at[c, j]).wait()
        for t in range(2):
            for m in range(4):
                for group in range(2):
                    values = [recv_a[c, j, 4 * group + k, t, m] for k in range(4)]
                    values = exchange(values, 32)
                    at = 256 * t + 128 * group
                    for pair in range(2):
                        high, low = split(
                            jnp.concatenate((values[2 * pair], values[2 * pair + 1]), 0)
                        )
                        here = 32 * m + 16 * pair
                        data_b[here : here + 16, at : at + 128] = high
                        data_b[here : here + 16, at + 512 : at + 640] = high
                        data_b[here : here + 16, at + 1024 : at + 1152] = low
        out = matmul_t(tb[...], data_b[...])
        for t in range(2):
            send_b[c, j, t] = out[256 * t : 256 * t + 256, :]

        def one(k, _):
            to = lax.rem(col + k, COLS)
            pltpu.make_async_remote_copy(
                src_ref=send_b.at[c, j, :, pl.ds(KZS * to, KZS), :],
                dst_ref=recv_b.at[j, col, c],
                send_sem=sb_sem,
                recv_sem=rb_sem.at[j],
                device_id={"col": to},
                device_id_type=MESH,
            ).start()
            return 0

        lax.fori_loop(1, COLS, one, 0)
        pltpu.make_async_copy(
            send_b.at[c, j, :, pl.ds(KZS * col, KZS), :], recv_b.at[j, col, c], rb_sem.at[j]
        ).start()
        return 0

    lax.fori_loop(0, 3 * PARTS, stage_b, 0)

    for load in loads[5:]:
        load.wait()
    grad_acc[...] = jnp.zeros_like(grad_acc)

    def stage_c(j, _):
        pltpu.make_async_copy(recv_b.at[j], recv_b.at[j], rb_sem.at[j]).wait()

        def gather(step, _):
            c = step // 2
            s = step % 2
            for group in range(2):
                values = [recv_b[j, 8 * group + k, c, s] for k in range(8)]
                values = exchange(values, 1)
                at = pl.multiple_of(256 * s + 128 * group, 128)
                for x in range(8):
                    high, low = split(values[x])
                    rows = pl.ds(pl.multiple_of(128 * c + 16 * x, 16), 16)
                    lhs_c[rows, pl.ds(at, 128)] = high
                    lhs_c[rows, pl.ds(at + 512, 128)] = high
                    lhs_c[rows, pl.ds(at + 1024, 128)] = low
            return 0

        lax.fori_loop(0, 6, gather, 0)
        work_c[...] = matmul(lhs_c[...], tc[...])

        def cross(i, _):
            there = pl.ds(pl.multiple_of(128 * j + 16 * i, 16), 16)
            adjoint = [work_c[pl.ds(pl.multiple_of(128 * c + 16 * i, 16), 16), :] for c in range(3)]
            for f in range(6):
                feature = feat[f, there, :]
                for c in range(3):
                    product = adjoint[c] * feature
                    total = (product[:8, :128] + product[:8, 128:]) + (
                        product[8:, :128] + product[8:, 128:]
                    )
                    grad_acc[6 * c + f] += total
            spin = [feat[3 + c, there, :] for c in range(3)]
            for c in range(3):
                second, third = (c + 1) % 3, (c + 2) % 3
                high, low = split(
                    spin[second] * adjoint[third] - spin[third] * adjoint[second]
                )
                rows = pl.ds(pl.multiple_of(128 * c + 16 * i, 16), 16)
                lhs_z[rows, 0:256] = high
                lhs_z[rows, 256:512] = high
                lhs_z[rows, 512:768] = low
            return 0

        lax.fori_loop(0, 8, cross, 0)
        work_z[...] = matmul(lhs_z[...], tz[...])

        def scatter(c, _):
            for n in range(3):
                values = [
                    work_z[
                        pl.ds(pl.multiple_of(128 * c + 16 * x, 16), 16), 128 * n : 128 * n + 128
                    ]
                    for x in range(8)
                ]
                values = exchange(values, 16)
                for b in range(8):
                    block = 8 * n + b
                    send_c[j, c, block >> 1, block & 1] = values[b]

            def one(slot, _):
                to = active_col(slot)
                mine = recv_c.at[j, c, :, pl.ds(KZS * col, KZS), :]

                @pl.when(to != col)
                def _():
                    pltpu.make_async_remote_copy(
                        src_ref=send_c.at[j, c, slot],
                        dst_ref=mine,
                        send_sem=sc_sem,
                        recv_sem=rc_sem.at[j, c],
                        device_id={"col": to},
                        device_id_type=MESH,
                    ).start()

                @pl.when(to == col)
                def _():
                    pltpu.make_async_copy(send_c.at[j, c, slot], mine, rc_sem.at[j, c]).start()

                return 0

            lax.fori_loop(0, NCOL, one, 0)
            return 0

        lax.fori_loop(0, 3, scatter, 0)
        return 0

    lax.fori_loop(0, PARTS, stage_c, 0)

    for k in range(18):
        grad_part[k : k + 1, :] = jnp.sum(grad_acc[k], axis=0, keepdims=True)
    grad_part[18:24, :] = jnp.zeros((6, 128), F32)

    def share_row(k, _):
        pltpu.make_async_remote_copy(
            src_ref=grad_part,
            dst_ref=grad_row.at[row],
            send_sem=grad_send.at[0],
            recv_sem=grad_recv.at[0],
            device_id={"row": lax.rem(row + k, ROWS)},
            device_id_type=MESH,
        ).start()
        return 0

    lax.fori_loop(1, ROWS, share_row, 0)
    pltpu.make_async_copy(grad_part, grad_row.at[row], grad_recv.at[0]).start()

    def stage_d(unit, _):
        j = unit // 3
        c = unit % 3

        @pl.when(col_active)
        def _():
            pltpu.make_async_copy(recv_c.at[j, c], recv_c.at[j, c], rc_sem.at[j, c]).wait()
            for s in range(2):
                high, low = split(recv_c[j, c, s])
                rhs[256 * s : 256 * s + 256, :] = high
                rhs[512 + 256 * s : 768 + 256 * s, :] = high
                rhs[1024 + 256 * s : 1280 + 256 * s, :] = low
            out = matmul(td[...], rhs[...])
            for slot in range(NROW):
                for t in range(2):
                    at = 64 * slot + 32 * t
                    send_d[j, c, slot, t] = out[at : at + 32, :]

            def one(slot, _):
                to = active_row(slot)

                @pl.when(to != row)
                def _():
                    pltpu.make_async_remote_copy(
                        src_ref=send_d.at[j, c, slot],
                        dst_ref=recv_d.at[j, c, row],
                        send_sem=sd_sem,
                        recv_sem=rd_sem.at[j, c],
                        device_id={"row": to},
                        device_id_type=MESH,
                    ).start()

                @pl.when(to == row)
                def _():
                    pltpu.make_async_copy(
                        send_d.at[j, c, slot], recv_d.at[j, c, row], rd_sem.at[j, c]
                    ).start()

                return 0

            lax.fori_loop(0, NROW, one, 0)

        return 0

    def stage_e(unit, _):
        j = unit // 3
        c = unit % 3

        @pl.when(col_active & row_active)
        def _():
            pltpu.make_async_copy(recv_d.at[j, c], recv_d.at[j, c], rd_sem.at[j, c]).wait()

            def gather(step, _):
                at = pl.multiple_of(16 * step, 16)
                values = [
                    recv_d[j, c, k & 7, k >> 3, pl.ds(at, 16), :] for k in range(16)
                ]
                values = exchange(values, 1)
                for kz in range(16):
                    high, low = split(values[kz])
                    rows = pl.ds(pl.multiple_of(KYS * kz + at, 16), 16)
                    lhs_e[rows, 0:128] = high
                    lhs_e[rows, 128:256] = high
                    lhs_e[rows, 256:384] = low
                return 0

            lax.fori_loop(0, 2, gather, 0)

            @pl.when(j == 0)
            def _():
                spec[c] = matmul(lhs_e[...], te[j])

            @pl.when(j > 0)
            def _():
                spec[c] += matmul(lhs_e[...], te[j])

            @pl.when(j == PARTS - 1)
            def _():
                pltpu.make_async_copy(spec.at[c], spec_out.at[c], out_sem).start()

        return 0

    lax.fori_loop(0, 9, stage_d, 0)

    pltpu.make_async_copy(grad_row, grad_row, grad_recv.at[0]).wait()
    grad_sum_row[...] = jnp.sum(grad_row[...], axis=0)

    def share_col(k, _):
        pltpu.make_async_remote_copy(
            src_ref=grad_sum_row,
            dst_ref=grad_col.at[col],
            send_sem=grad_send.at[1],
            recv_sem=grad_recv.at[1],
            device_id={"col": lax.rem(col + k, COLS)},
            device_id_type=MESH,
        ).start()
        return 0

    lax.fori_loop(1, COLS, share_col, 0)
    pltpu.make_async_copy(grad_sum_row, grad_col.at[col], grad_recv.at[1]).start()

    lax.fori_loop(0, 9, stage_e, 0)

    pltpu.make_async_copy(grad_col, grad_col, grad_recv.at[1]).wait()
    grad_sum_col[...] = jnp.sum(grad_col[...], axis=0)
    pltpu.make_async_remote_copy(
        src_ref=grad_sum_col,
        dst_ref=grad_env.at[env],
        send_sem=grad_send.at[2],
        recv_sem=grad_recv.at[2],
        device_id={"env": 1 - env},
        device_id_type=MESH,
    ).start()
    pltpu.make_async_copy(grad_sum_col, grad_env.at[env], grad_recv.at[2]).start()

    lax.fori_loop(9, 12, stage_d, 0)

    pltpu.make_async_copy(grad_env, grad_env, grad_recv.at[2]).wait()
    total = jnp.sum(grad_env[0] + grad_env[1], axis=1, keepdims=True)
    total = total * (1.0 / math.sqrt(2 * N**3))
    grad_out[...] = jnp.broadcast_to(total, (24, 128))

    def sent(ref, sem):
        pltpu.make_async_copy(ref, ref, sem).wait()

    for j in range(PARTS):
        for c in range(3):
            sent(send_a.at[c, j, pl.ds(0, ROWS - 1)], sa_sem)
            sent(recv_b.at[j, pl.ds(0, COLS - 1), c], sb_sem)

    @pl.when(col_active)
    def _():
        for j in range(PARTS):
            for c in range(3):
                sent(send_c.at[j, c, pl.ds(0, NCOL - 1)], sc_sem)

    @pl.when(jnp.logical_not(col_active))
    def _():
        sent(send_c, sc_sem)

    sent(grad_row.at[pl.ds(0, ROWS - 1)], grad_send.at[0])
    sent(grad_col.at[pl.ds(0, COLS - 1)], grad_send.at[1])
    sent(grad_env.at[0], grad_send.at[2])

    lax.fori_loop(9, 12, stage_e, 0)

    @pl.when(col_active)
    def _():
        @pl.when(row_active)
        def _():
            for j in range(PARTS):
                for c in range(3):
                    sent(send_d.at[j, c, pl.ds(0, NROW - 1)], sd_sem)
            sent(spec, out_sem)

        @pl.when(jnp.logical_not(row_active))
        def _():
            sent(send_d, sd_sem)


def last_body(spec, out, work):
    row = lax.axis_index("row")
    col = lax.axis_index("col")
    tile = pl.program_id(0)
    active = ((col < 6) | (col >= 10)) & ((row < 3) | (row >= 5))

    @pl.when(jnp.logical_not(active))
    def _():
        out[...] = jnp.zeros_like(out)

    @pl.when(active)
    def _():
        def signed(index):
            return jnp.where(index < N // 2, index, index - N).astype(F32)

        wave_x = signed(lax.broadcasted_iota(jnp.int32, (8, 256), 1))
        wave_y = signed(
            lax.broadcasted_iota(jnp.int32, (8, 256), 0) + (KYS * row + 8 * tile)
        )
        kept_xy = (3.0 * jnp.abs(wave_x) < N) & (3.0 * jnp.abs(wave_y) < N)
        square_xy = wave_x * wave_x + wave_y * wave_y

        def project(kz, _):
            wave_z = signed(jnp.full((8, 256), KZS * col + kz, jnp.int32))
            kept = kept_xy & (3.0 * jnp.abs(wave_z) < N)
            square = jnp.maximum(square_xy + wave_z * wave_z, 1.0)
            inverse = 1.0 / square
            waves = (wave_x, wave_y, wave_z)
            for t in range(2):
                parts = [spec[c, kz, :, 256 * t : 256 * t + 256] for c in range(3)]
                inner = (
                    wave_x * parts[0] + wave_y * parts[1] + wave_z * parts[2]
                ) * inverse
                for c in range(3):
                    value = jnp.where(kept, parts[c] - waves[c] * inner, 0.0)
                    for lanes in range(2):
                        work[c, t, lanes, pl.ds(kz, 8, stride=16), :] = value[
                            :, 128 * lanes : 128 * lanes + 128
                        ]
            return 0

        lax.fori_loop(0, 16, project, 0)
        for c in range(3):
            for t in range(2):
                for lanes in range(2):
                    out[c, t, :, 128 * lanes : 128 * lanes + 128] = work[c, t, lanes]


def shards(adjoint_hat, velocity, vorticity):
    constants = [jnp.asarray(t) for t in tables()]
    hbm = pl.BlockSpec(memory_space=pl.ANY)
    vmem = pltpu.VMEM
    dma = pltpu.SemaphoreType.DMA
    spec, grad = pl.pallas_call(
        body,
        name="advect",
        out_shape=(
            jax.ShapeDtypeStruct((3, 512, 512), F32),
            jax.ShapeDtypeStruct((24, 128), F32),
        ),
        in_specs=[hbm] * 9,
        out_specs=(hbm, pl.BlockSpec(memory_space=pltpu.VMEM)),
        scratch_shapes=[
            vmem((3, 2, KZS, KYS, 256), F32),
            vmem((6, 512, 256), F32),
            vmem((512, 1536), BF16),
            vmem((512, 1536), BF16),
            vmem((1536, 256), BF16),
            vmem((768, 384), BF16),
            vmem((384, 1536), BF16),
            vmem((PARTS, 384, 512), BF16),
            vmem((512, 1536), BF16),
            vmem((3, PARTS, ROWS, 2, 4, 8, 128), F32),
            vmem((3, PARTS, ROWS, 2, 4, 8, 128), F32),
            vmem((128, 1536), BF16),
            vmem((3, PARTS, 2, N, 128), F32),
            vmem((PARTS, COLS, 3, 2, KZS, 128), F32),
            vmem((384, 1536), BF16),
            vmem((384, 256), F32),
            vmem((384, 768), BF16),
            vmem((384, 384), F32),
            vmem((PARTS, 3, NCOL, 2, KZS, 128), F32),
            vmem((PARTS, 3, 2, N, 128), F32),
            vmem((1536, 128), BF16),
            vmem((PARTS, 3, NROW, 2, KYS, 128), F32),
            vmem((PARTS, 3, ROWS, 2, KYS, 128), F32),
            vmem((512, 384), BF16),
            vmem((3, 512, 512), F32),
            vmem((18, 8, 128), F32),
            vmem((24, 128), F32),
            vmem((ROWS, 24, 128), F32),
            vmem((24, 128), F32),
            vmem((COLS, 24, 128), F32),
            vmem((24, 128), F32),
            vmem((2, 24, 128), F32),
            dma((11,)),
            dma((3, PARTS)),
            dma((PARTS,)),
            dma((PARTS, 3)),
            dma((PARTS, 3)),
            dma,
            dma,
            dma,
            dma,
            dma((3,)),
            dma((3,)),
            dma,
        ],
        compiler_params=pltpu.CompilerParams(
            collective_id=0, has_side_effects=True, vmem_limit_bytes=60 * 2**20
        ),
    )(
        adjoint_hat[0],
        velocity.reshape(3, 512, 256),
        vorticity.reshape(3, 512, 256),
        *constants,
    )
    out = pl.pallas_call(
        last_body,
        name="project",
        grid=(4,),
        out_shape=jax.ShapeDtypeStruct((3, 2, 512, 256), F32),
        in_specs=[pl.BlockSpec((3, KZS, 8, 512), lambda i: (0, 0, i, 0))],
        out_specs=pl.BlockSpec((3, 2, 128, 256), lambda i: (0, 0, i, 0)),
        scratch_shapes=[vmem((3, 2, 2, 128, 128), F32)],
        compiler_params=pltpu.CompilerParams(vmem_limit_bytes=40 * 2**20),
    )(spec.reshape(3, KZS, KYS, 512))
    return out.reshape(adjoint_hat.shape), grad[:18, 0].reshape(3, 6)


def solution(mesh):
    placed = (
        P("env", None, None, "row", "col", None),
        P("env", None, "row", "col", None),
        P("env", None, "row", "col", None),
    )
    return jax.shard_map(
        shards,
        mesh=mesh,
        in_specs=placed,
        out_specs=(P("env", None, None, "row", "col", None), P()),
        check_vma=False,
    )
```

time: 207 us -> 183 us (0.88)
  Pallas kernels: 203 us -> 180 us
    pallas_call x1, Pallas kernels: 188 us -> 175 us  [shards(): pl.pallas_call(body, name='advect', out_shape=(jax.ShapeDtypeStruct((3, 5...]
    pallas_call x1, Pallas kernels: 15 us -> 4.06 us  [shards(): pl.pallas_call(last_body, name='project', grid=(4,), out_shape=jax.ShapeD...]
where the time goes in v2:
time: 183 us
  Pallas kernels  180 us (98%)
  local copies, waits for them, and re-layouts  2.67 us (1%)
    pallas_call x1, Pallas kernels, shards(): pl.pallas_call(body, name='advect', out_shape=(jax.ShapeDtypeStruct((3, 5...  175 us
    pallas_call x1, Pallas kernels, shards(): pl.pallas_call(last_body, name='project', grid=(4,), out_shape=jax.ShapeD...  4.06 us

profile of v2, /device:TPU:1, one launch (start us, length us, event | category | flops | bytes accessed | tf_op | source)
XLA Modules:
  0.0 182.8 jit_solution(2978550637704615070)
XLA Ops:
  0.6 175.5 %advect.1 = (f32[3,512,512]{2,1,0:T(8,128)}, f32[24,128]{1,0:T(8,128)}) custom-call(f32[3,2,32,16,256]{4,3,2,1,0:T(8,128)} %bitcast.7, f32[3,512,256]{2,1,0:T(8,128)} %bitcast.8, f32[3,512,256]{2,1,0:T(8,128)} %bitcast.9, bf16[512,1536]{1,0:T(8,128)(2,1)} %constant.12.clone.ta_hbm, bf16[512,1536]{1,0:T(8,128)(2,1)} %constant.13.clone.tb_hbm, ...), custom_call_target="tpu_custom_call" | custom-call | tf_op jit(solution)/shard_map/advect/pallas_call | solution.py:596
  176.1 0.0 copy-start
  176.1 1.9 %copy-done = f32[3,512,512]{2,1,0:T(8,128)S(1)} copy-done((f32[3,512,512]{2,1,0:T(8,128)S(1)}, f32[3,512,512]{2,1,0:T(8,128)}, u32[]{:S(2)}) %copy-start) | copy-done | bytes 3145752
  178.0 0.0 copy-start.1
  178.0 4.1 %project.1 = f32[3,2,512,256]{3,2,1,0:T(8,128)} custom-call(f32[3,16,32,512]{3,2,1,0:T(8,128)S(1)} %bitcast.5), custom_call_target="tpu_custom_call" | custom-call | tf_op jit(solution)/shard_map/project/pallas_call | solution.py:660
  182.1 0.0 copy-done.1
  182.1 0.1 slice_reduce_fusion
  182.2 0.7 reshape_squeeze.3
Async XLA Ops:
  176.1 1.9 %copy-start = (f32[3,512,512]{2,1,0:T(8,128)S(1)}, f32[3,512,512]{2,1,0:T(8,128)}, u32[]{:S(2)}) copy-start(f32[3,512,512]{2,1,0:T(8,128)} %get-tuple-element.4) | copy-start | bytes 9437188
  178.0 4.1 %copy-start.1 = (f32[24,128]{1,0:T(8,128)S(1)}, f32[24,128]{1,0:T(8,128)}, u32[]{:S(2)}) copy-start(f32[24,128]{1,0:T(8,128)} %get-tuple-element.5) | copy-start | bytes 36868

commit v3 on v2

--- a/solution.py
+++ b/solution.py
@@ -19,6 +19,8 @@
 KYS = 32
 KZS = 16
 PARTS = 4
+WINDOW_B = 2
+WINDOW_C = 2
 ACTIVE_COLS = (0, 1, 2, 3, 4, 5, 10, 11, 12, 13, 14, 15)
 ACTIVE_ROWS = (0, 1, 2, 5, 6, 7)
 NCOL = len(ACTIVE_COLS)
@@ -116,12 +118,18 @@
     )
 
 
-def active_col(slot):
-    return jnp.where(slot < 6, slot, slot + 4)
-
-
-def active_row(slot):
-    return jnp.where(slot < 3, slot, slot + 2)
+def offset(k, size):
+    step = k
+    away = step // 2 + 1
+    return jnp.where(step % 2 == 0, away, size - away)
+
+
+def is_active_col(col):
+    return (col < 6) | (col >= 10)
+
+
+def is_active_row(row):
+    return (row < 3) | (row >= 5)
 
 
 def body(
@@ -137,8 +145,8 @@
     env = lax.axis_index("env")
     row = lax.axis_index("row")
     col = lax.axis_index("col")
-    col_active = (col < 6) | (col >= 10)
-    row_active = (row < 3) | (row >= 5)
+    col_active = is_active_col(col)
+    row_active = is_active_row(row)
 
     barrier = pltpu.get_barrier_semaphore()
 
@@ -160,10 +168,9 @@
 
     def load_g(c):
         def one(kz, _):
-            for s in range(2):
-                pltpu.make_async_copy(
-                    g_hbm.at[c, s, :, kz, :], g.at[c, s, kz], load_sem.at[1 + c]
-                ).start()
+            pltpu.make_async_copy(
+                g_hbm.at[c, :, :, kz, :], g.at[c, kz], load_sem.at[1 + c]
+            ).start()
             return 0
 
         lax.fori_loop(0, KZS, one, 0)
@@ -178,16 +185,14 @@
     loads.append(pltpu.make_async_copy(tz_hbm, tz, load_sem.at[8]))
     loads.append(pltpu.make_async_copy(td_hbm, td, load_sem.at[9]))
     loads.append(pltpu.make_async_copy(te_hbm, te, load_sem.at[10]))
+    loads[0].start()
     load_g(0)
-    loads[0].start()
+    loads[4].start()
     load_g(1)
-    load_g(2)
-    for load in loads[4:]:
-        load.start()
 
     def start_row(c, j):
         def one(k, _):
-            to = lax.rem(row + k, ROWS)
+            to = lax.rem(row + offset(k, ROWS), ROWS)
             pltpu.make_async_remote_copy(
                 src_ref=send_a.at[c, j, to],
                 dst_ref=recv_a.at[c, j, row],
@@ -198,13 +203,13 @@
             ).start()
             return 0
 
-        lax.fori_loop(1, ROWS, one, 0)
+        lax.fori_loop(0, ROWS - 1, one, 0)
         pltpu.make_async_copy(send_a.at[c, j, row], recv_a.at[c, j, row], ra_sem.at[c, j]).start()
 
     for c in range(3):
         loads[1 + c].wait()
         for s in range(2):
-            high, low = split(g[c, s].reshape(512, 256))
+            high, low = split(g[c, :, s].reshape(512, 256))
             data_a[:, 256 * s : 256 * s + 256] = high
             data_a[:, 512 + 256 * s : 768 + 256 * s] = high
             data_a[:, 1024 + 256 * s : 1280 + 256 * s] = low
@@ -224,8 +229,27 @@
                 pl.semaphore_wait(barrier, ROWS - 1 + COLS - 1 + 1)
             start_row(c, 2 * half)
             start_row(c, 2 * half + 1)
+        if c == 0:
+            load_g(2)
+            for load in loads[5:]:
+                load.start()
 
     loads[4].wait()
+
+    def sent(ref, sem):
+        pltpu.make_async_copy(ref, ref, sem).wait()
+
+    def sent_b(unit):
+        sent(recv_b.at[0, pl.ds(0, COLS - 1), 0], sb_sem.at[unit])
+
+    def sent_c(unit):
+        @pl.when(col_active)
+        def _():
+            sent(send_c.at[0, 0, pl.ds(0, NCOL - 1)], sc_sem.at[unit])
+
+        @pl.when(jnp.logical_not(col_active))
+        def _():
+            sent(send_c.at[0, 0], sc_sem.at[unit])
 
     def stage_b(unit, _):
         c = unit // PARTS
@@ -249,19 +273,23 @@
         for t in range(2):
             send_b[c, j, t] = out[256 * t : 256 * t + 256, :]
 
+        @pl.when(unit >= WINDOW_B)
+        def _():
+            sent_b(unit - WINDOW_B)
+
         def one(k, _):
-            to = lax.rem(col + k, COLS)
+            to = lax.rem(col + offset(k, COLS), COLS)
             pltpu.make_async_remote_copy(
                 src_ref=send_b.at[c, j, :, pl.ds(KZS * to, KZS), :],
                 dst_ref=recv_b.at[j, col, c],
-                send_sem=sb_sem,
+                send_sem=sb_sem.at[unit],
                 recv_sem=rb_sem.at[j],
                 device_id={"col": to},
                 device_id_type=MESH,
             ).start()
             return 0
 
-        lax.fori_loop(1, COLS, one, 0)
+        lax.fori_loop(0, COLS - 1, one, 0)
         pltpu.make_async_copy(
             send_b.at[c, j, :, pl.ds(KZS * col, KZS), :], recv_b.at[j, col, c], rb_sem.at[j]
         ).start()
@@ -333,52 +361,41 @@
                     block = 8 * n + b
                     send_c[j, c, block >> 1, block & 1] = values[b]
 
-            def one(slot, _):
-                to = active_col(slot)
-                mine = recv_c.at[j, c, :, pl.ds(KZS * col, KZS), :]
-
-                @pl.when(to != col)
+            unit = 3 * j + c
+
+            @pl.when(unit >= WINDOW_C)
+            def _():
+                sent_c(unit - WINDOW_C)
+
+            mine = recv_c.at[j, c, :, pl.ds(KZS * col, KZS), :]
+
+            def one(k, _):
+                to = lax.rem(col + offset(k, COLS), COLS)
+
+                @pl.when(is_active_col(to))
                 def _():
                     pltpu.make_async_remote_copy(
-                        src_ref=send_c.at[j, c, slot],
+                        src_ref=send_c.at[j, c, jnp.where(to < 6, to, to - 4)],
                         dst_ref=mine,
-                        send_sem=sc_sem,
+                        send_sem=sc_sem.at[unit],
                         recv_sem=rc_sem.at[j, c],
                         device_id={"col": to},
                         device_id_type=MESH,
                     ).start()
 
-                @pl.when(to == col)
-                def _():
-                    pltpu.make_async_copy(send_c.at[j, c, slot], mine, rc_sem.at[j, c]).start()
-
                 return 0
 
-            lax.fori_loop(0, NCOL, one, 0)
+            lax.fori_loop(0, COLS - 1, one, 0)
+
+            @pl.when(col_active)
+            def _():
+                own = send_c.at[j, c, jnp.where(col < 6, col, col - 4)]
+                pltpu.make_async_copy(own, mine, rc_sem.at[j, c]).start()
+
             return 0
 
         lax.fori_loop(0, 3, scatter, 0)
         return 0
-
-    lax.fori_loop(0, PARTS, stage_c, 0)
-
-    for k in range(18):
-        grad_part[k : k + 1, :] = jnp.sum(grad_acc[k], axis=0, keepdims=True)
-    grad_part[18:24, :] = jnp.zeros((6, 128), F32)
-
-    def share_row(k, _):
-        pltpu.make_async_remote_copy(
-            src_ref=grad_part,
-            dst_ref=grad_row.at[row],
-            send_sem=grad_send.at[0],
-            recv_sem=grad_recv.at[0],
-            device_id={"row": lax.rem(row + k, ROWS)},
-            device_id_type=MESH,
-        ).start()
-        return 0
-
-    lax.fori_loop(1, ROWS, share_row, 0)
-    pltpu.make_async_copy(grad_part, grad_row.at[row], grad_recv.at[0]).start()
 
     def stage_d(unit, _):
         j = unit // 3
@@ -398,29 +415,30 @@
                     at = 64 * slot + 32 * t
                     send_d[j, c, slot, t] = out[at : at + 32, :]
 
-            def one(slot, _):
-                to = active_row(slot)
-
-                @pl.when(to != row)
+            mine = recv_d.at[j, c, row]
+
+            def one(k, _):
+                to = lax.rem(row + offset(k, ROWS), ROWS)
+
+                @pl.when(is_active_row(to))
                 def _():
                     pltpu.make_async_remote_copy(
-                        src_ref=send_d.at[j, c, slot],
-                        dst_ref=recv_d.at[j, c, row],
+                        src_ref=send_d.at[j, c, jnp.where(to < 3, to, to - 2)],
+                        dst_ref=mine,
                         send_sem=sd_sem,
                         recv_sem=rd_sem.at[j, c],
                         device_id={"row": to},
                         device_id_type=MESH,
                     ).start()
 
-                @pl.when(to == row)
-                def _():
-                    pltpu.make_async_copy(
-                        send_d.at[j, c, slot], recv_d.at[j, c, row], rd_sem.at[j, c]
-                    ).start()
-
                 return 0
 
-            lax.fori_loop(0, NROW, one, 0)
+            lax.fori_loop(0, ROWS - 1, one, 0)
+
+            @pl.when(row_active)
+            def _():
+                own = send_d.at[j, c, jnp.where(row < 3, row, row - 2)]
+                pltpu.make_async_copy(own, mine, rd_sem.at[j, c]).start()
 
         return 0
 
@@ -462,7 +480,34 @@
 
         return 0
 
-    lax.fori_loop(0, 9, stage_d, 0)
+    stage_c(0, 0)
+    stage_c(1, 0)
+    lax.fori_loop(0, 3, stage_d, 0)
+    stage_c(2, 0)
+    lax.fori_loop(3, 6, stage_d, 0)
+    lax.fori_loop(0, 3, stage_e, 0)
+    stage_c(3, 0)
+
+    for k in range(18):
+        grad_part[k : k + 1, :] = jnp.sum(grad_acc[k], axis=0, keepdims=True)
+    grad_part[18:24, :] = jnp.zeros((6, 128), F32)
+
+    def share_row(k, _):
+        pltpu.make_async_remote_copy(
+            src_ref=grad_part,
+            dst_ref=grad_row.at[row],
+            send_sem=grad_send.at[0],
+            recv_sem=grad_recv.at[0],
+            device_id={"row": lax.rem(row + k, ROWS)},
+            device_id_type=MESH,
+        ).start()
+        return 0
+
+    lax.fori_loop(1, ROWS, share_row, 0)
+    pltpu.make_async_copy(grad_part, grad_row.at[row], grad_recv.at[0]).start()
+
+    lax.fori_loop(6, 9, stage_d, 0)
+    lax.fori_loop(3, 6, stage_e, 0)
 
     pltpu.make_async_copy(grad_row, grad_row, grad_recv.at[0]).wait()
     grad_sum_row[...] = jnp.sum(grad_row[...], axis=0)
@@ -481,7 +526,10 @@
     lax.fori_loop(1, COLS, share_col, 0)
     pltpu.make_async_copy(grad_sum_row, grad_col.at[col], grad_recv.at[1]).start()
 
-    lax.fori_loop(0, 9, stage_e, 0)
+    stage_d(9, 0)
+    lax.fori_loop(6, 9, stage_e, 0)
+    stage_d(10, 0)
+    stage_e(9, 0)
 
     pltpu.make_async_copy(grad_col, grad_col, grad_recv.at[1]).wait()
     grad_sum_col[...] = jnp.sum(grad_col[...], axis=0)
@@ -495,36 +543,31 @@
     ).start()
     pltpu.make_async_copy(grad_sum_col, grad_env.at[env], grad_recv.at[2]).start()
 
-    lax.fori_loop(9, 12, stage_d, 0)
+    stage_d(11, 0)
+    stage_e(10, 0)
 
     pltpu.make_async_copy(grad_env, grad_env, grad_recv.at[2]).wait()
     total = jnp.sum(grad_env[0] + grad_env[1], axis=1, keepdims=True)
     total = total * (1.0 / math.sqrt(2 * N**3))
-    grad_out[...] = jnp.broadcast_to(total, (24, 128))
-
-    def sent(ref, sem):
-        pltpu.make_async_copy(ref, ref, sem).wait()
-
-    for j in range(PARTS):
-        for c in range(3):
+    lane = lax.broadcasted_iota(jnp.int32, (1, 6), 1)
+    for c in range(3):
+        line = jnp.zeros((1, 6), F32)
+        for f in range(6):
+            line = jnp.where(lane == f, total[6 * c + f : 6 * c + f + 1, :], line)
+        grad_out[c : c + 1, :] = line
+
+    for c in range(3):
+        for j in range(PARTS):
             sent(send_a.at[c, j, pl.ds(0, ROWS - 1)], sa_sem)
-            sent(recv_b.at[j, pl.ds(0, COLS - 1), c], sb_sem)
-
-    @pl.when(col_active)
-    def _():
-        for j in range(PARTS):
-            for c in range(3):
-                sent(send_c.at[j, c, pl.ds(0, NCOL - 1)], sc_sem)
-
-    @pl.when(jnp.logical_not(col_active))
-    def _():
-        sent(send_c, sc_sem)
-
+    for unit in range(3 * PARTS - WINDOW_B, 3 * PARTS):
+        sent_b(unit)
+    for unit in range(3 * PARTS - WINDOW_C, 3 * PARTS):
+        sent_c(unit)
     sent(grad_row.at[pl.ds(0, ROWS - 1)], grad_send.at[0])
     sent(grad_col.at[pl.ds(0, COLS - 1)], grad_send.at[1])
     sent(grad_env.at[0], grad_send.at[2])
 
-    lax.fori_loop(9, 12, stage_e, 0)
+    stage_e(11, 0)
 
     @pl.when(col_active)
     def _():
@@ -540,52 +583,70 @@
             sent(send_d, sd_sem)
 
 
-def last_body(spec, out, work):
+def last_body(spec, sums, out, grad, before, after, in_sem, out_sem):
     row = lax.axis_index("row")
     col = lax.axis_index("col")
-    tile = pl.program_id(0)
-    active = ((col < 6) | (col >= 10)) & ((row < 3) | (row >= 5))
+    active = is_active_col(col) & is_active_row(row)
+    grad[...] = sums[...]
+
+    def leave(kz, source):
+        pltpu.make_async_copy(after.at[source], out.at[:, :, :, kz, :], out_sem).start()
 
     @pl.when(jnp.logical_not(active))
     def _():
-        out[...] = jnp.zeros_like(out)
+        after[0] = jnp.zeros(after.shape[1:], F32)
+
+        def one(kz, _):
+            leave(kz, 0)
+            return 0
+
+        lax.fori_loop(0, KZS, one, 0)
 
     @pl.when(active)
     def _():
+        def enter(kz, _):
+            pltpu.make_async_copy(spec.at[:, kz], before.at[kz], in_sem.at[kz]).start()
+            return 0
+
+        lax.fori_loop(0, KZS, enter, 0)
+
         def signed(index):
             return jnp.where(index < N // 2, index, index - N).astype(F32)
 
         wave_x = signed(lax.broadcasted_iota(jnp.int32, (8, 256), 1))
-        wave_y = signed(
-            lax.broadcasted_iota(jnp.int32, (8, 256), 0) + (KYS * row + 8 * tile)
-        )
-        kept_xy = (3.0 * jnp.abs(wave_x) < N) & (3.0 * jnp.abs(wave_y) < N)
-        square_xy = wave_x * wave_x + wave_y * wave_y
+        lines = lax.broadcasted_iota(jnp.int32, (8, 256), 0)
 
         def project(kz, _):
+            pltpu.make_async_copy(before.at[kz], before.at[kz], in_sem.at[kz]).wait()
             wave_z = signed(jnp.full((8, 256), KZS * col + kz, jnp.int32))
-            kept = kept_xy & (3.0 * jnp.abs(wave_z) < N)
-            square = jnp.maximum(square_xy + wave_z * wave_z, 1.0)
-            inverse = 1.0 / square
-            waves = (wave_x, wave_y, wave_z)
-            for t in range(2):
-                parts = [spec[c, kz, :, 256 * t : 256 * t + 256] for c in range(3)]
-                inner = (
-                    wave_x * parts[0] + wave_y * parts[1] + wave_z * parts[2]
-                ) * inverse
-                for c in range(3):
-                    value = jnp.where(kept, parts[c] - waves[c] * inner, 0.0)
-                    for lanes in range(2):
-                        work[c, t, lanes, pl.ds(kz, 8, stride=16), :] = value[
-                            :, 128 * lanes : 128 * lanes + 128
-                        ]
-            return 0
-
-        lax.fori_loop(0, 16, project, 0)
-        for c in range(3):
-            for t in range(2):
-                for lanes in range(2):
-                    out[c, t, :, 128 * lanes : 128 * lanes + 128] = work[c, t, lanes]
+            for tile in range(4):
+                wave_y = signed(lines + (KYS * row + 8 * tile))
+                kept = (
+                    (3.0 * jnp.abs(wave_x) < N)
+                    & (3.0 * jnp.abs(wave_y) < N)
+                    & (3.0 * jnp.abs(wave_z) < N)
+                )
+                square = wave_x * wave_x + wave_y * wave_y + wave_z * wave_z
+                inverse = 1.0 / jnp.maximum(square, 1.0)
+                waves = (wave_x, wave_y, wave_z)
+                here = slice(8 * tile, 8 * tile + 8)
+                for t in range(2):
+                    parts = [
+                        before[kz, c, here, 256 * t : 256 * t + 256] for c in range(3)
+                    ]
+                    inner = (
+                        wave_x * parts[0] + wave_y * parts[1] + wave_z * parts[2]
+                    ) * inverse
+                    for c in range(3):
+                        after[kz, c, t, here, :] = jnp.where(
+                            kept, parts[c] - waves[c] * inner, 0.0
+                        )
+            leave(kz, kz)
+            return 0
+
+        lax.fori_loop(0, KZS, project, 0)
+
+    pltpu.make_async_copy(after, after, out_sem).wait()
 
 
 def shards(adjoint_hat, velocity, vorticity):
@@ -598,12 +659,12 @@
         name="advect",
         out_shape=(
             jax.ShapeDtypeStruct((3, 512, 512), F32),
-            jax.ShapeDtypeStruct((24, 128), F32),
+            jax.ShapeDtypeStruct((3, 6), F32),
         ),
         in_specs=[hbm] * 9,
         out_specs=(hbm, pl.BlockSpec(memory_space=pltpu.VMEM)),
         scratch_shapes=[
-            vmem((3, 2, KZS, KYS, 256), F32),
+            vmem((3, KZS, 2, KYS, 256), F32),
             vmem((6, 512, 256), F32),
             vmem((512, 1536), BF16),
             vmem((512, 1536), BF16),
@@ -641,8 +702,8 @@
             dma((PARTS, 3)),
             dma((PARTS, 3)),
             dma,
-            dma,
-            dma,
+            dma((3 * PARTS,)),
+            dma((3 * PARTS,)),
             dma,
             dma((3,)),
             dma((3,)),
@@ -657,17 +718,24 @@
         vorticity.reshape(3, 512, 256),
         *constants,
     )
-    out = pl.pallas_call(
+    out, grad = pl.pallas_call(
         last_body,
         name="project",
-        grid=(4,),
-        out_shape=jax.ShapeDtypeStruct((3, 2, 512, 256), F32),
-        in_specs=[pl.BlockSpec((3, KZS, 8, 512), lambda i: (0, 0, i, 0))],
-        out_specs=pl.BlockSpec((3, 2, 128, 256), lambda i: (0, 0, i, 0)),
-        scratch_shapes=[vmem((3, 2, 2, 128, 128), F32)],
-        compiler_params=pltpu.CompilerParams(vmem_limit_bytes=40 * 2**20),
-    )(spec.reshape(3, KZS, KYS, 512))
-    return out.reshape(adjoint_hat.shape), grad[:18, 0].reshape(3, 6)
+        out_shape=(
+            jax.ShapeDtypeStruct((3, 2, KYS, KZS, N), F32),
+            jax.ShapeDtypeStruct((3, 6), F32),
+        ),
+        in_specs=[hbm, pl.BlockSpec(memory_space=pltpu.VMEM)],
+        out_specs=(hbm, pl.BlockSpec(memory_space=pltpu.VMEM)),
+        scratch_shapes=[
+            vmem((KZS, 3, KYS, 512), F32),
+            vmem((KZS, 3, 2, KYS, N), F32),
+            dma((KZS,)),
+            dma,
+        ],
+        compiler_params=pltpu.CompilerParams(vmem_limit_bytes=60 * 2**20),
+    )(spec.reshape(3, KZS, KYS, 512), grad)
+    return out.reshape(adjoint_hat.shape), grad
 
 
 def solution(mesh):

time: 183 us -> 174 us (0.951)
  Pallas kernels: 180 us -> 173 us
  local copies, waits for them, and re-layouts: 2.67 us -> 0 us
    pallas_call x1, Pallas kernels: 175 us -> 169 us  [shards(): pl.pallas_call(body, name='advect', out_shape=(jax.ShapeDtypeStruct((3, 5...]
    unnamed x4 -> x0, local copies, waits for them, and re-layouts: 1.89 us -> none
where the time goes in v3:
time: 174 us
  Pallas kernels  173 us (99%)
    pallas_call x1, Pallas kernels, shards(): pl.pallas_call(body, name='advect', out_shape=(jax.ShapeDtypeStruct((3, 5...  169 us
    pallas_call x1, Pallas kernels, shards(): pl.pallas_call(last_body, name='project', out_shape=(jax.ShapeDtypeStruct...  4.23 us

profile of v3, /device:TPU:1, one launch (start us, length us, event | category | flops | bytes accessed | tf_op | source)
XLA Modules:
  0.0 174.0 jit_solution(5946325028192427978)
XLA Ops:
  0.6 169.2 %advect.1 = (f32[3,512,512]{2,1,0:T(8,128)}, f32[3,6]{1,0:T(4,128)}) custom-call(f32[3,2,32,16,256]{4,3,2,1,0:T(8,128)} %bitcast.6, f32[3,512,256]{2,1,0:T(8,128)} %bitcast.7, f32[3,512,256]{2,1,0:T(8,128)} %bitcast.8, bf16[512,1536]{1,0:T(8,128)(2,1)} %constant.12.clone.ta_hbm, bf16[512,1536]{1,0:T(8,128)(2,1)} %constant.13.clone.tb_hbm, ...), custom_call_target="tpu_custom_call" | custom-call | tf_op jit(solution)/shard_map/advect/pallas_call | solution.py:657
  169.8 4.2 %project.1 = (f32[3,2,32,16,256]{4,3,2,1,0:T(8,128)}, f32[3,6]{1,0:T(4,128)}) custom-call(f32[3,16,32,512]{3,2,1,0:T(8,128)} %bitcast.5, f32[3,6]{1,0:T(4,128)} %get-tuple-element.7.sums), custom_call_target="tpu_custom_call" | custom-call | tf_op jit(solution)/shard_map/project/pallas_call | solution.py:721

commit v4 on v3

--- a/solution.py
+++ b/solution.py
@@ -148,24 +148,6 @@
     col_active = is_active_col(col)
     row_active = is_active_row(row)
 
-    barrier = pltpu.get_barrier_semaphore()
-
-    def greet_row(k, _):
-        pl.semaphore_signal(
-            barrier, inc=1, device_id={"row": lax.rem(row + k, ROWS)}, device_id_type=MESH
-        )
-        return 0
-
-    def greet_col(k, _):
-        pl.semaphore_signal(
-            barrier, inc=1, device_id={"col": lax.rem(col + k, COLS)}, device_id_type=MESH
-        )
-        return 0
-
-    lax.fori_loop(1, ROWS, greet_row, 0)
-    lax.fori_loop(1, COLS, greet_col, 0)
-    pl.semaphore_signal(barrier, inc=1, device_id={"env": 1 - env}, device_id_type=MESH)
-
     def load_g(c):
         def one(kz, _):
             pltpu.make_async_copy(
@@ -175,20 +157,41 @@
 
         lax.fori_loop(0, KZS, one, 0)
 
-    loads = [pltpu.make_async_copy(ta_hbm, ta, load_sem.at[0])]
+    half_a = pl.ds(0, 256)
+    loads = [pltpu.make_async_copy(ta_hbm.at[half_a], ta.at[half_a], load_sem.at[0])]
     for c in range(3):
         loads.append(pltpu.make_async_copy(g.at[c], g.at[c], load_sem.at[1 + c]))
     loads.append(pltpu.make_async_copy(tb_hbm, tb, load_sem.at[4]))
+    half_a = pl.ds(256, 256)
+    loads.append(pltpu.make_async_copy(ta_hbm.at[half_a], ta.at[half_a], load_sem.at[11]))
     loads.append(pltpu.make_async_copy(tc_hbm, tc, load_sem.at[5]))
     loads.append(pltpu.make_async_copy(vel_hbm, feat.at[pl.ds(0, 3)], load_sem.at[6]))
     loads.append(pltpu.make_async_copy(vort_hbm, feat.at[pl.ds(3, 3)], load_sem.at[7]))
     loads.append(pltpu.make_async_copy(tz_hbm, tz, load_sem.at[8]))
     loads.append(pltpu.make_async_copy(td_hbm, td, load_sem.at[9]))
     loads.append(pltpu.make_async_copy(te_hbm, te, load_sem.at[10]))
+    load_g(0)
     loads[0].start()
-    load_g(0)
+    barrier = pltpu.get_barrier_semaphore()
+
+    def greet_row(k, _):
+        pl.semaphore_signal(
+            barrier, inc=1, device_id={"row": lax.rem(row + k, ROWS)}, device_id_type=MESH
+        )
+        return 0
+
+    def greet_col(k, _):
+        pl.semaphore_signal(
+            barrier, inc=1, device_id={"col": lax.rem(col + k, COLS)}, device_id_type=MESH
+        )
+        return 0
+
+    lax.fori_loop(1, ROWS, greet_row, 0)
+    lax.fori_loop(1, COLS, greet_col, 0)
+    pl.semaphore_signal(barrier, inc=1, device_id={"env": 1 - env}, device_id_type=MESH)
+
+    load_g(1)
     loads[4].start()
-    load_g(1)
 
     def start_row(c, j):
         def one(k, _):
@@ -206,35 +209,42 @@
         lax.fori_loop(0, ROWS - 1, one, 0)
         pltpu.make_async_copy(send_a.at[c, j, row], recv_a.at[c, j, row], ra_sem.at[c, j]).start()
 
-    for c in range(3):
+    def load_data(c):
         loads[1 + c].wait()
         for s in range(2):
             high, low = split(g[c, :, s].reshape(512, 256))
             data_a[:, 256 * s : 256 * s + 256] = high
             data_a[:, 512 + 256 * s : 768 + 256 * s] = high
             data_a[:, 1024 + 256 * s : 1280 + 256 * s] = low
-        if c == 0:
-            loads[0].wait()
-        for half in range(2):
-            out = matmul_t(ta[256 * half : 256 * half + 256, :], data_a[...])
-            for part in range(2):
-                for t in range(2):
-                    for r in range(ROWS):
-                        at = 128 * part + 64 * t + 8 * r
-                        for m in range(4):
-                            send_a[c, 2 * half + part, r, t, m] = out[
-                                at : at + 8, 128 * m : 128 * m + 128
-                            ]
-            if c == 0 and half == 0:
-                pl.semaphore_wait(barrier, ROWS - 1 + COLS - 1 + 1)
-            start_row(c, 2 * half)
-            start_row(c, 2 * half + 1)
-        if c == 0:
-            load_g(2)
-            for load in loads[5:]:
-                load.start()
-
-    loads[4].wait()
+
+    def stage_a(c, half):
+        out = matmul_t(ta[256 * half : 256 * half + 256, :], data_a[...])
+        for part in range(2):
+            for t in range(2):
+                for r in range(ROWS):
+                    at = 128 * part + 64 * t + 8 * r
+                    for m in range(4):
+                        send_a[c, 2 * half + part, r, t, m] = out[
+                            at : at + 8, 128 * m : 128 * m + 128
+                        ]
+
+    load_data(0)
+    loads[0].wait()
+    stage_a(0, 0)
+    pl.semaphore_wait(barrier, ROWS - 1 + COLS - 1 + 1)
+    start_row(0, 0)
+    start_row(0, 1)
+    loads[5].start()
+    load_g(2)
+    loads[5].wait()
+    stage_a(0, 1)
+    start_row(0, 2)
+    start_row(0, 3)
+    for load in loads[6:]:
+        load.start()
+    load_data(1)
+    stage_a(1, 0)
+    stage_a(1, 1)
 
     def sent(ref, sem):
         pltpu.make_async_copy(ref, ref, sem).wait()
@@ -295,11 +305,104 @@
         ).start()
         return 0
 
-    lax.fori_loop(0, 3 * PARTS, stage_b, 0)
-
-    for load in loads[5:]:
+    loads[4].wait()
+    stage_b(0, 0)
+    for part in range(PARTS):
+        start_row(1, part)
+    stage_b(1, 0)
+    load_data(2)
+    stage_a(2, 0)
+    stage_a(2, 1)
+    for part in range(PARTS):
+        start_row(2, part)
+    lax.fori_loop(2, 3 * PARTS, stage_b, 0)
+
+    for load in loads[6:]:
         load.wait()
     grad_acc[...] = jnp.zeros_like(grad_acc)
+
+    def stage_d(unit, _):
+        j = unit // 3
+        c = unit % 3
+
+        @pl.when(col_active)
+        def _():
+            pltpu.make_async_copy(recv_c.at[j, c], recv_c.at[j, c], rc_sem.at[j, c]).wait()
+            for s in range(2):
+                high, low = split(recv_c[j, c, s])
+                rhs[256 * s : 256 * s + 256, :] = high
+                rhs[512 + 256 * s : 768 + 256 * s, :] = high
+                rhs[1024 + 256 * s : 1280 + 256 * s, :] = low
+            out = matmul(td[...], rhs[...])
+            for slot in range(NROW):
+                for t in range(2):
+                    at = 64 * slot + 32 * t
+                    send_d[j, c, slot, t] = out[at : at + 32, :]
+
+            mine = recv_d.at[j, c, row]
+
+            def one(k, _):
+                to = lax.rem(row + offset(k, ROWS), ROWS)
+
+                @pl.when(is_active_row(to))
+                def _():
+                    pltpu.make_async_remote_copy(
+                        src_ref=send_d.at[j, c, jnp.where(to < 3, to, to - 2)],
+                        dst_ref=mine,
+                        send_sem=sd_sem,
+                        recv_sem=rd_sem.at[j, c],
+                        device_id={"row": to},
+                        device_id_type=MESH,
+                    ).start()
+
+                return 0
+
+            lax.fori_loop(0, ROWS - 1, one, 0)
+
+            @pl.when(row_active)
+            def _():
+                own = send_d.at[j, c, jnp.where(row < 3, row, row - 2)]
+                pltpu.make_async_copy(own, mine, rd_sem.at[j, c]).start()
+
+        return 0
+
+    def stage_e(unit, _):
+        j = unit // 3
+        c = unit % 3
+
+        @pl.when(col_active & row_active)
+        def _():
+            pltpu.make_async_copy(recv_d.at[j, c], recv_d.at[j, c], rd_sem.at[j, c]).wait()
+
+            def gather(step, _):
+                at = pl.multiple_of(16 * step, 16)
+                values = [
+                    recv_d[j, c, k & 7, k >> 3, pl.ds(at, 16), :] for k in range(16)
+                ]
+                values = exchange(values, 1)
+                for kz in range(16):
+                    high, low = split(values[kz])
+                    rows = pl.ds(pl.multiple_of(KYS * kz + at, 16), 16)
+                    lhs_e[rows, 0:128] = high
+                    lhs_e[rows, 128:256] = high
+                    lhs_e[rows, 256:384] = low
+                return 0
+
+            lax.fori_loop(0, 2, gather, 0)
+
+            @pl.when(j == 0)
+            def _():
+                spec[c] = matmul(lhs_e[...], te[j])
+
+            @pl.when(j > 0)
+            def _():
+                spec[c] += matmul(lhs_e[...], te[j])
+
+            @pl.when(j == PARTS - 1)
+            def _():
+                pltpu.make_async_copy(spec.at[c], spec_out.at[c], out_sem).start()
+
+        return 0
 
     def stage_c(j, _):
         pltpu.make_async_copy(recv_b.at[j], recv_b.at[j], rb_sem.at[j]).wait()
@@ -397,89 +500,6 @@
         lax.fori_loop(0, 3, scatter, 0)
         return 0
 
-    def stage_d(unit, _):
-        j = unit // 3
-        c = unit % 3
-
-        @pl.when(col_active)
-        def _():
-            pltpu.make_async_copy(recv_c.at[j, c], recv_c.at[j, c], rc_sem.at[j, c]).wait()
-            for s in range(2):
-                high, low = split(recv_c[j, c, s])
-                rhs[256 * s : 256 * s + 256, :] = high
-                rhs[512 + 256 * s : 768 + 256 * s, :] = high
-                rhs[1024 + 256 * s : 1280 + 256 * s, :] = low
-            out = matmul(td[...], rhs[...])
-            for slot in range(NROW):
-                for t in range(2):
-                    at = 64 * slot + 32 * t
-                    send_d[j, c, slot, t] = out[at : at + 32, :]
-
-            mine = recv_d.at[j, c, row]
-
-            def one(k, _):
-                to = lax.rem(row + offset(k, ROWS), ROWS)
-
-                @pl.when(is_active_row(to))
-                def _():
-                    pltpu.make_async_remote_copy(
-                        src_ref=send_d.at[j, c, jnp.where(to < 3, to, to - 2)],
-                        dst_ref=mine,
-                        send_sem=sd_sem,
-                        recv_sem=rd_sem.at[j, c],
-                        device_id={"row": to},
-                        device_id_type=MESH,
-                    ).start()
-
-                return 0
-
-            lax.fori_loop(0, ROWS - 1, one, 0)
-
-            @pl.when(row_active)
-            def _():
-                own = send_d.at[j, c, jnp.where(row < 3, row, row - 2)]
-                pltpu.make_async_copy(own, mine, rd_sem.at[j, c]).start()
-
-        return 0
-
-    def stage_e(unit, _):
-        j = unit // 3
-        c = unit % 3
-
-        @pl.when(col_active & row_active)
-        def _():
-            pltpu.make_async_copy(recv_d.at[j, c], recv_d.at[j, c], rd_sem.at[j, c]).wait()
-
-            def gather(step, _):
-                at = pl.multiple_of(16 * step, 16)
-                values = [
-                    recv_d[j, c, k & 7, k >> 3, pl.ds(at, 16), :] for k in range(16)
-                ]
-                values = exchange(values, 1)
-                for kz in range(16):
-                    high, low = split(values[kz])
-                    rows = pl.ds(pl.multiple_of(KYS * kz + at, 16), 16)
-                    lhs_e[rows, 0:128] = high
-                    lhs_e[rows, 128:256] = high
-                    lhs_e[rows, 256:384] = low
-                return 0
-
-            lax.fori_loop(0, 2, gather, 0)
-
-            @pl.when(j == 0)
-            def _():
-                spec[c] = matmul(lhs_e[...], te[j])
-
-            @pl.when(j > 0)
-            def _():
-                spec[c] += matmul(lhs_e[...], te[j])
-
-            @pl.when(j == PARTS - 1)
-            def _():
-                pltpu.make_async_copy(spec.at[c], spec_out.at[c], out_sem).start()
-
-        return 0
-
     stage_c(0, 0)
     stage_c(1, 0)
     lax.fori_loop(0, 3, stage_d, 0)
@@ -506,9 +526,15 @@
     lax.fori_loop(1, ROWS, share_row, 0)
     pltpu.make_async_copy(grad_part, grad_row.at[row], grad_recv.at[0]).start()
 
+    sent(send_a.at[:, :, pl.ds(0, ROWS - 1)], sa_sem)
+    for unit in range(3 * PARTS - WINDOW_B, 3 * PARTS):
+        sent_b(unit)
+
     lax.fori_loop(6, 9, stage_d, 0)
     lax.fori_loop(3, 6, stage_e, 0)
-
+    stage_d(9, 0)
+    lax.fori_loop(6, 8, stage_e, 0)
+    stage_d(10, 0)
     pltpu.make_async_copy(grad_row, grad_row, grad_recv.at[0]).wait()
     grad_sum_row[...] = jnp.sum(grad_row[...], axis=0)
 
@@ -526,11 +552,8 @@
     lax.fori_loop(1, COLS, share_col, 0)
     pltpu.make_async_copy(grad_sum_row, grad_col.at[col], grad_recv.at[1]).start()
 
-    stage_d(9, 0)
-    lax.fori_loop(6, 9, stage_e, 0)
-    stage_d(10, 0)
-    stage_e(9, 0)
-
+    stage_e(8, 0)
+    stage_d(11, 0)
     pltpu.make_async_copy(grad_col, grad_col, grad_recv.at[1]).wait()
     grad_sum_col[...] = jnp.sum(grad_col[...], axis=0)
     pltpu.make_async_remote_copy(
@@ -543,9 +566,8 @@
     ).start()
     pltpu.make_async_copy(grad_sum_col, grad_env.at[env], grad_recv.at[2]).start()
 
-    stage_d(11, 0)
+    stage_e(9, 0)
     stage_e(10, 0)
-
     pltpu.make_async_copy(grad_env, grad_env, grad_recv.at[2]).wait()
     total = jnp.sum(grad_env[0] + grad_env[1], axis=1, keepdims=True)
     total = total * (1.0 / math.sqrt(2 * N**3))
@@ -556,11 +578,6 @@
             line = jnp.where(lane == f, total[6 * c + f : 6 * c + f + 1, :], line)
         grad_out[c : c + 1, :] = line
 
-    for c in range(3):
-        for j in range(PARTS):
-            sent(send_a.at[c, j, pl.ds(0, ROWS - 1)], sa_sem)
-    for unit in range(3 * PARTS - WINDOW_B, 3 * PARTS):
-        sent_b(unit)
     for unit in range(3 * PARTS - WINDOW_C, 3 * PARTS):
         sent_c(unit)
     sent(grad_row.at[pl.ds(0, ROWS - 1)], grad_send.at[0])
@@ -573,9 +590,7 @@
     def _():
         @pl.when(row_active)
         def _():
-            for j in range(PARTS):
-                for c in range(3):
-                    sent(send_d.at[j, c, pl.ds(0, NROW - 1)], sd_sem)
+            sent(send_d.at[:, :, pl.ds(0, NROW - 1)], sd_sem)
             sent(spec, out_sem)
 
         @pl.when(jnp.logical_not(row_active))
@@ -696,7 +711,7 @@
             vmem((COLS, 24, 128), F32),
             vmem((24, 128), F32),
             vmem((2, 24, 128), F32),
-            dma((11,)),
+            dma((12,)),
             dma((3, PARTS)),
             dma((PARTS,)),
             dma((PARTS, 3)),

time: 174 us -> 173 us (level)
  no operation moved by 1% of the time
where the time goes in v4:
time: 173 us
  Pallas kernels  172 us (99%)
    pallas_call x1, Pallas kernels, shards(): pl.pallas_call(body, name='advect', out_shape=(jax.ShapeDtypeStruct((3, 5...  168 us
    pallas_call x1, Pallas kernels, shards(): pl.pallas_call(last_body, name='project', out_shape=(jax.ShapeDtypeStruct...  4.23 us

profile of v4, /device:TPU:1, one launch (start us, length us, event | category | flops | bytes accessed | tf_op | source)
XLA Modules:
  0.0 172.7 jit_solution(4377980026731750101)
XLA Ops:
  0.6 167.8 %advect.1 = (f32[3,512,512]{2,1,0:T(8,128)}, f32[3,6]{1,0:T(4,128)}) custom-call(f32[3,2,32,16,256]{4,3,2,1,0:T(8,128)} %bitcast.6, f32[3,512,256]{2,1,0:T(8,128)} %bitcast.7, f32[3,512,256]{2,1,0:T(8,128)} %bitcast.8, bf16[512,1536]{1,0:T(8,128)(2,1)} %constant.12.clone.ta_hbm, bf16[512,1536]{1,0:T(8,128)(2,1)} %constant.13.clone.tb_hbm, ...), custom_call_target="tpu_custom_call" | custom-call | tf_op jit(solution)/shard_map/advect/pallas_call | solution.py:672
  168.4 4.2 %project.1 = (f32[3,2,32,16,256]{4,3,2,1,0:T(8,128)}, f32[3,6]{1,0:T(4,128)}) custom-call(f32[3,16,32,512]{3,2,1,0:T(8,128)} %bitcast.5, f32[3,6]{1,0:T(4,128)} %get-tuple-element.7.sums), custom_call_target="tpu_custom_call" | custom-call | tf_op jit(solution)/shard_map/project/pallas_call | solution.py:736

commit v5 on v4

--- a/solution.py
+++ b/solution.py
@@ -19,6 +19,7 @@
 KYS = 32
 KZS = 16
 PARTS = 4
+TILES = 8
 WINDOW_B = 2
 WINDOW_C = 2
 ACTIVE_COLS = (0, 1, 2, 3, 4, 5, 10, 11, 12, 13, 14, 15)
@@ -400,7 +401,14 @@
 
             @pl.when(j == PARTS - 1)
             def _():
-                pltpu.make_async_copy(spec.at[c], spec_out.at[c], out_sem).start()
+                def leave(kz, _):
+                    rows = pl.ds(pl.multiple_of(KYS * kz, KYS), KYS)
+                    pltpu.make_async_copy(
+                        spec.at[c, rows], spec_out.at[c, :, kz, :], out_sem
+                    ).start()
+                    return 0
+
+                lax.fori_loop(0, KZS, leave, 0)
 
         return 0
 
@@ -604,62 +612,70 @@
     active = is_active_col(col) & is_active_row(row)
     grad[...] = sums[...]
 
-    def leave(kz, source):
-        pltpu.make_async_copy(after.at[source], out.at[:, :, :, kz, :], out_sem).start()
+    lines = KYS // TILES
+
+    def leave(tile, source):
+        pltpu.make_async_copy(
+            after.at[source], out.at[:, :, pl.ds(lines * tile, lines)], out_sem
+        ).start()
 
     @pl.when(jnp.logical_not(active))
     def _():
         after[0] = jnp.zeros(after.shape[1:], F32)
 
-        def one(kz, _):
-            leave(kz, 0)
-            return 0
-
-        lax.fori_loop(0, KZS, one, 0)
+        def one(tile, _):
+            leave(tile, 0)
+            return 0
+
+        lax.fori_loop(0, TILES, one, 0)
 
     @pl.when(active)
     def _():
-        def enter(kz, _):
-            pltpu.make_async_copy(spec.at[:, kz], before.at[kz], in_sem.at[kz]).start()
-            return 0
-
-        lax.fori_loop(0, KZS, enter, 0)
+        def enter(tile, _):
+            pltpu.make_async_copy(
+                spec.at[:, pl.ds(lines * tile, lines)], before.at[tile], in_sem.at[tile]
+            ).start()
+            return 0
+
+        lax.fori_loop(0, TILES, enter, 0)
 
         def signed(index):
             return jnp.where(index < N // 2, index, index - N).astype(F32)
 
         wave_x = signed(lax.broadcasted_iota(jnp.int32, (8, 256), 1))
-        lines = lax.broadcasted_iota(jnp.int32, (8, 256), 0)
-
-        def project(kz, _):
-            pltpu.make_async_copy(before.at[kz], before.at[kz], in_sem.at[kz]).wait()
-            wave_z = signed(jnp.full((8, 256), KZS * col + kz, jnp.int32))
-            for tile in range(4):
-                wave_y = signed(lines + (KYS * row + 8 * tile))
-                kept = (
-                    (3.0 * jnp.abs(wave_x) < N)
-                    & (3.0 * jnp.abs(wave_y) < N)
-                    & (3.0 * jnp.abs(wave_z) < N)
-                )
-                square = wave_x * wave_x + wave_y * wave_y + wave_z * wave_z
-                inverse = 1.0 / jnp.maximum(square, 1.0)
-                waves = (wave_x, wave_y, wave_z)
-                here = slice(8 * tile, 8 * tile + 8)
-                for t in range(2):
-                    parts = [
-                        before[kz, c, here, 256 * t : 256 * t + 256] for c in range(3)
-                    ]
-                    inner = (
-                        wave_x * parts[0] + wave_y * parts[1] + wave_z * parts[2]
-                    ) * inverse
-                    for c in range(3):
-                        after[kz, c, t, here, :] = jnp.where(
-                            kept, parts[c] - waves[c] * inner, 0.0
-                        )
-            leave(kz, kz)
-            return 0
-
-        lax.fori_loop(0, KZS, project, 0)
+        down = lax.broadcasted_iota(jnp.int32, (8, 256), 0)
+
+        def project(tile, _):
+            pltpu.make_async_copy(before.at[tile], before.at[tile], in_sem.at[tile]).wait()
+            for line in range(lines):
+                wave_y = signed(jnp.full((8, 256), KYS * row + lines * tile + line, jnp.int32))
+                for part in range(2):
+                    wave_z = signed(down + (KZS * col + 8 * part))
+                    kept = (
+                        (3.0 * jnp.abs(wave_x) < N)
+                        & (3.0 * jnp.abs(wave_y) < N)
+                        & (3.0 * jnp.abs(wave_z) < N)
+                    )
+                    square = wave_x * wave_x + wave_y * wave_y + wave_z * wave_z
+                    inverse = 1.0 / jnp.maximum(square, 1.0)
+                    waves = (wave_x, wave_y, wave_z)
+                    here = slice(8 * part, 8 * part + 8)
+                    for t in range(2):
+                        parts = [
+                            before[tile, c, line, here, 256 * t : 256 * t + 256]
+                            for c in range(3)
+                        ]
+                        inner = (
+                            wave_x * parts[0] + wave_y * parts[1] + wave_z * parts[2]
+                        ) * inverse
+                        for c in range(3):
+                            after[tile, c, t, line, here, :] = jnp.where(
+                                kept, parts[c] - waves[c] * inner, 0.0
+                            )
+            leave(tile, tile)
+            return 0
+
+        lax.fori_loop(0, TILES, project, 0)
 
     pltpu.make_async_copy(after, after, out_sem).wait()
 
@@ -673,7 +689,7 @@
         body,
         name="advect",
         out_shape=(
-            jax.ShapeDtypeStruct((3, 512, 512), F32),
+            jax.ShapeDtypeStruct((3, KYS, KZS, 512), F32),
             jax.ShapeDtypeStruct((3, 6), F32),
         ),
         in_specs=[hbm] * 9,
@@ -743,13 +759,13 @@
         in_specs=[hbm, pl.BlockSpec(memory_space=pltpu.VMEM)],
         out_specs=(hbm, pl.BlockSpec(memory_space=pltpu.VMEM)),
         scratch_shapes=[
-            vmem((KZS, 3, KYS, 512), F32),
-            vmem((KZS, 3, 2, KYS, N), F32),
-            dma((KZS,)),
+            vmem((TILES, 3, KYS // TILES, KZS, 512), F32),
+            vmem((TILES, 3, 2, KYS // TILES, KZS, N), F32),
+            dma((TILES,)),
             dma,
         ],
         compiler_params=pltpu.CompilerParams(vmem_limit_bytes=60 * 2**20),
-    )(spec.reshape(3, KZS, KYS, 512), grad)
+    )(spec, grad)
     return out.reshape(adjoint_hat.shape), grad
 
 

time: 173 us -> 174 us (level)
  no operation moved by 1% of the time
where the time goes in v5:
time: 174 us; the launch traced here: 173 us
  Pallas kernels  172 us (99%)
    pallas_call x1, Pallas kernels, shards(): pl.pallas_call(body, name='advect', out_shape=(jax.ShapeDtypeStruct((3, K...  168 us
    pallas_call x1, Pallas kernels, shards(): pl.pallas_call(last_body, name='project', out_shape=(jax.ShapeDtypeStruct...  4.07 us

profile of v5, /device:TPU:1, one launch (start us, length us, event | category | flops | bytes accessed | tf_op | source)
XLA Modules:
  0.0 173.1 jit_solution(12791101076692707049)
XLA Ops:
  0.6 168.3 %advect.1 = (f32[3,32,16,512]{3,2,1,0:T(8,128)}, f32[3,6]{1,0:T(4,128)}) custom-call(f32[3,2,32,16,256]{4,3,2,1,0:T(8,128)} %bitcast.4, f32[3,512,256]{2,1,0:T(8,128)} %bitcast.5, f32[3,512,256]{2,1,0:T(8,128)} %bitcast.6, bf16[512,1536]{1,0:T(8,128)(2,1)} %constant.12.clone.ta_hbm, bf16[512,1536]{1,0:T(8,128)(2,1)} %constant.13.clone.tb_hbm, ...), custom_call_target="tpu_custom_call" | custom-call | tf_op jit(solution)/shard_map/advect/pallas_call | solution.py:688
  168.9 4.1 %project.1 = (f32[3,2,32,16,256]{4,3,2,1,0:T(8,128)}, f32[3,6]{1,0:T(4,128)}) custom-call(f32[3,32,16,512]{3,2,1,0:T(8,128)} %get-tuple-element.6.spec, f32[3,6]{1,0:T(4,128)} %get-tuple-element.7.sums), custom_call_target="tpu_custom_call" | custom-call | tf_op jit(solution)/shard_map/project/pallas_call | solution.py:752

commit v6 on v4

--- a/solution.py
+++ b/solution.py
@@ -473,9 +473,9 @@
             mine = recv_c.at[j, c, :, pl.ds(KZS * col, KZS), :]
 
             def one(k, _):
-                to = lax.rem(col + offset(k, COLS), COLS)
-
-                @pl.when(is_active_col(to))
+                to = lax.rem(col + offset(lax.rem(k, COLS - 1), COLS), COLS)
+
+                @pl.when(jnp.where(k < COLS - 1, to < 6, to >= 10))
                 def _():
                     pltpu.make_async_remote_copy(
                         src_ref=send_c.at[j, c, jnp.where(to < 6, to, to - 4)],
@@ -488,7 +488,7 @@
 
                 return 0
 
-            lax.fori_loop(0, COLS - 1, one, 0)
+            lax.fori_loop(0, 2 * (COLS - 1), one, 0)
 
             @pl.when(col_active)
             def _():

time: 173 us -> 173 us (level)
  no operation moved by 1% of the time
where the time goes in v6:
time: 173 us
  Pallas kernels  173 us (100%)
    pallas_call x1, Pallas kernels, shards(): pl.pallas_call(body, name='advect', out_shape=(jax.ShapeDtypeStruct((3, 5...  168 us
    pallas_call x1, Pallas kernels, shards(): pl.pallas_call(last_body, name='project', out_shape=(jax.ShapeDtypeStruct...  4.23 us

profile of v6, /device:TPU:1, one launch (start us, length us, event | category | flops | bytes accessed | tf_op | source)
XLA Modules:
  0.0 173.3 jit_solution(10560683401521113592)
XLA Ops:
  0.6 168.4 %advect.1 = (f32[3,512,512]{2,1,0:T(8,128)}, f32[3,6]{1,0:T(4,128)}) custom-call(f32[3,2,32,16,256]{4,3,2,1,0:T(8,128)} %bitcast.6, f32[3,512,256]{2,1,0:T(8,128)} %bitcast.7, f32[3,512,256]{2,1,0:T(8,128)} %bitcast.8, bf16[512,1536]{1,0:T(8,128)(2,1)} %constant.12.clone.ta_hbm, bf16[512,1536]{1,0:T(8,128)(2,1)} %constant.13.clone.tb_hbm, ...), custom_call_target="tpu_custom_call" | custom-call | tf_op jit(solution)/shard_map/advect/pallas_call | solution.py:672
  169.1 4.2 %project.1 = (f32[3,2,32,16,256]{4,3,2,1,0:T(8,128)}, f32[3,6]{1,0:T(4,128)}) custom-call(f32[3,16,32,512]{3,2,1,0:T(8,128)} %bitcast.5, f32[3,6]{1,0:T(4,128)} %get-tuple-element.7.sums), custom_call_target="tpu_custom_call" | custom-call | tf_op jit(solution)/shard_map/project/pallas_call | solution.py:736
